TPU v7x, 128 devices: a whole 4x4x4 slice. The times are simulated.
128 devices in a mesh: seq: 32 (over z, y, core), head: 4 (over x).
Axes of the slice: x: 4, y: 4, z: 4, core: 2. Of those that a mesh axis runs over, the one named last changes fastest.
Arguments:
- queries: bfloat16 [32768, 2560], P(('seq', 'head'))
- keys: bfloat16 [32768, 2560], P(('seq', 'head'))
- values: bfloat16 [32768, 2560], P(('seq', 'head')), may hold values from -6 to 6
- gain_q: float32 [2560], replicated, may hold values from 0.1 to 1.9
- gain_k: float32 [2560], replicated, may hold values from 0.1 to 1.9
- key_tiles: int32 [256, 18], replicated, may hold values from 0 to 255, as said below
- tile_counts: int32 [256], replicated, may hold values from 1 to 18
- tile_valid: int32 [256], replicated, may hold values from 1 to 128, as said below
Outputs:
- attended: bfloat16 [32768, 2560], P(('seq', 'head'))
Inputs may be any that keep to these rules, and one draw needn't show every extreme that they name: `key_tiles`: entry 0 of row i is i and entry 1 is the other tile of the pair (2 m, 2 m + 1) holding i; the entries of a row are distinct tiles. Counting blocks of 8 tiles, the used entries of all rows of one block name at most one tile of each other block. `tile_valid`: every tile but the last one is full.
All inputs are finite; a program needn't handle non-finite values.
Results may differ from a plain program's by a relative error of at most 0.0072.
Values may be sent and summed in bfloat16 or wider, within the bound.
A program may use at most 192 MiB of HBM per device.

v0:
```python
import math

import jax
import jax.numpy as jnp
from jax import lax
from jax.sharding import PartitionSpec as P

HD = 128
TILE = 128


eps_norm = 1e-06


def head_major(rows, tile_count, heads_here):
    return rows.reshape(tile_count, TILE, heads_here, HD).transpose(2, 0, 1, 3)


def tile_attention(query_block, key_block, value_block, keep):
    scores = jnp.einsum(
        "hqad,hqkbd->hqakb", query_block, key_block, preferred_element_type=jnp.float32
    ) * HD ** (-0.5)
    scores = jnp.where(keep[None, :, None, :, :], scores, -1e30)
    peak = jnp.max(scores, axis=(3, 4), keepdims=True)
    weights = jnp.exp(scores - peak).astype(jnp.bfloat16)
    total = jnp.sum(weights.astype(jnp.float32), axis=(3, 4))
    mixed = jnp.einsum(
        "hqakb,hqkbd->hqad", weights, value_block, preferred_element_type=jnp.float32
    )
    return (mixed / total[..., None]).astype(jnp.bfloat16)


def on_device(queries, keys, values, gain_q, gain_k, key_tiles, tile_counts, tile_valid):
    head_count = lax.axis_size("head")
    seq_count = lax.axis_size("seq")
    tok_rows, width = queries.shape
    group_width = width // head_count
    heads_here = group_width // HD
    span_tiles = head_count * tok_rows // TILE
    slots = key_tiles.shape[1]
    span_id = lax.axis_index("seq")
    q_raw, k_raw, v_here = (
        lax.all_to_all(queries, "head", split_axis=1, concat_axis=0, tiled=True),
        lax.all_to_all(keys, "head", split_axis=1, concat_axis=0, tiled=True),
        lax.all_to_all(values, "head", split_axis=1, concat_axis=0, tiled=True),
    )
    q_float = q_raw.astype(jnp.float32)
    k_float = k_raw.astype(jnp.float32)
    q_square, k_square = lax.psum(
        (jnp.sum(q_float * q_float, axis=1), jnp.sum(k_float * k_float, axis=1)), "head"
    )
    offset = lax.axis_index("head") * group_width
    gain_q_here = lax.dynamic_slice_in_dim(gain_q, offset, group_width)
    gain_k_here = lax.dynamic_slice_in_dim(gain_k, offset, group_width)
    q_here = (q_float * lax.rsqrt(q_square / width + eps_norm)[:, None] * gain_q_here).astype(
        jnp.bfloat16
    )
    k_here = (k_float * lax.rsqrt(k_square / width + eps_norm)[:, None] * gain_k_here).astype(
        jnp.bfloat16
    )
    grid = key_tiles.reshape(seq_count, span_tiles, slots)
    used = (
        jnp.arange(slots, dtype=jnp.int32)[None, None, :]
        < tile_counts.reshape(seq_count, span_tiles)[:, :, None]
    )
    owner_all = grid // span_tiles
    others = jnp.arange(seq_count, dtype=jnp.int32)[:, None, None] != span_id
    match = used & (owner_all == span_id) & others
    wanted = jnp.max(jnp.where(match, grid % span_tiles, 0), axis=(1, 2))
    k_local = head_major(k_here, span_tiles, heads_here)
    v_local = head_major(v_here, span_tiles, heads_here)
    out_k = jnp.take(k_local, wanted, axis=1)
    out_v = jnp.take(v_local, wanted, axis=1)
    fetched_k, fetched_v = (
        lax.all_to_all(out_k, "seq", split_axis=1, concat_axis=1, tiled=True),
        lax.all_to_all(out_v, "seq", split_axis=1, concat_axis=1, tiled=True),
    )
    bank_k = jnp.concatenate([k_local, fetched_k], axis=1)
    bank_v = jnp.concatenate([v_local, fetched_v], axis=1)
    my_rows = lax.dynamic_slice_in_dim(key_tiles, span_id * span_tiles, span_tiles, 0)
    my_counts = lax.dynamic_slice_in_dim(tile_counts, span_id * span_tiles, span_tiles, 0)
    owner_mine = my_rows // span_tiles
    bank_index = jnp.where(owner_mine == span_id, my_rows % span_tiles, span_tiles + owner_mine)
    valid_here = jnp.take(tile_valid, my_rows)
    keep = (jnp.arange(slots, dtype=jnp.int32)[None, :, None] < my_counts[:, None, None]) & (
        jnp.arange(TILE, dtype=jnp.int32)[None, None, :] < valid_here[:, :, None]
    )
    block = math.gcd(span_tiles, 4)
    blocks = span_tiles // block
    q_tiles = q_here.reshape(blocks, block, TILE, heads_here, HD).transpose(0, 3, 1, 2, 4)

    def attend(inputs):
        q_block, index_block, keep_block = inputs
        k_block = jnp.take(bank_k, index_block, axis=1)
        v_block = jnp.take(bank_v, index_block, axis=1)
        return tile_attention(q_block, k_block, v_block, keep_block)

    result = lax.map(
        attend,
        (
            q_tiles,
            bank_index.reshape(blocks, block, slots),
            keep.reshape(blocks, block, slots, TILE),
        ),
    )
    mixed = result.transpose(0, 2, 3, 1, 4).reshape(span_tiles * TILE, group_width)
    return lax.all_to_all(mixed, "head", split_axis=0, concat_axis=1, tiled=True)


def solution(mesh):
    placed = (
        P(("seq", "head"), None),
        P(("seq", "head"), None),
        P(("seq", "head"), None),
        P(),
        P(),
        P(),
        P(),
        P(),
    )
    return jax.shard_map(
        on_device, mesh=mesh, in_specs=placed, out_specs=P(("seq", "head"), None), check_vma=False
    )
```

profile of v0, /device:TPU:1, one launch (start us, length us, event | category | flops | bytes accessed | tf_op | source)
XLA Modules:
  0.0 383.9 jit_solution(8745930475474575289)
XLA Ops:
  2.5 4.8 %all-to-all-start = ((bf16[256,4,640]{0,2,1:T(8,128)(2,1)}), bf16[256,4,640]{0,2,1:T(8,128)(2,1)S(1)}, u32[]{:S(2)}, u32[]{:S(2)}) async-start(bf16[256,4,640]{0,2,1:T(8,128)(2,1)} %bitcast.13), calls=%async_computation | async-start | bytes 2621440 | tf_op jit(solution)/shard_map/all_to_all | solution.py:43
  8.8 15.6 %all-to-all-done = bf16[256,4,640]{0,2,1:T(8,128)(2,1)S(1)} async-done(((bf16[256,4,640]{0,2,1:T(8,128)(2,1)}), bf16[256,4,640]{0,2,1:T(8,128)(2,1)S(1)}, u32[]{:S(2)}, u32[]{:S(2)}) %all-to-all-start) | async-done | bytes 1310752 | tf_op jit(solution)/shard_map/all_to_all | solution.py:43
  24.4 3.5 all-to-all-start.1
  31.2 12.8 %all-to-all-done.1 = bf16[256,4,640]{0,2,1:T(8,128)(2,1)S(1)} async-done(((bf16[256,4,640]{0,2,1:T(8,128)(2,1)}), bf16[256,4,640]{0,2,1:T(8,128)(2,1)S(1)}, u32[]{:S(2)}, u32[]{:S(2)}) %all-to-all-start.1) | async-done | bytes 1310752 | tf_op jit(solution)/shard_map/all_to_all | solution.py:44
  44.0 4.3 %all-to-all-start.3 = ((bf16[256,4,640]{0,2,1:T(8,128)(2,1)}), bf16[256,4,640]{0,2,1:T(8,128)(2,1)}, u32[]{:S(2)}, u32[]{:S(2)}) async-start(bf16[256,4,640]{0,2,1:T(8,128)(2,1)} %bitcast.109), calls=%async_computation.3 | async-start | bytes 2621440 | tf_op jit(solution)/shard_map/all_to_all | solution.py:45
  52.6 2.6 copy.54
  55.2 11.8 %all-reduce = (f32[1024]{0:T(1024)S(1)}, f32[1024]{0:T(1024)S(1)}) all-reduce(f32[1024]{0:T(1024)S(1)} %bitcast.116, f32[1024]{0:T(1024)S(1)} %bitcast.117), channel_id=1, replica_groups=mesh['seq'=32,'head'=4] {'head'}, use_global_device_ids=true, to_apply=%region_1.0 | all-reduce | flops 2048 | bytes 16384 | tf_op jit(solution)/shard_map/psum | solution.py:49
  74.6 3.6 gather_fusion.3
  78.2 3.5 gather_fusion.4
  81.7 8.9 %select_bitcast_fusion = (bf16[5,32,128,128]{3,2,0,1:T(8,128)(2,1)}, bf16[5,32,128,128]{3,2,0,1:T(8,128)(2,1)}) fusion(bf16[32,5,128,128]{3,2,1,0:T(8,128)(2,1)} %gather_fusion.4, pred[32]{0:T(512)(128)(4,1)S(1)} %compare_and_fusion.1, bf16[32,5,128,128]{3,2,1,0:T(8,128)(2,1)} %gather_fusion.3), kind=kLoop, calls=%fused_computation.35 | loop fusion | flops 5242880 | bytes 20971552 | tf_op jit(solution)/shard_map/jit(_take)/select_n | solution.py:73
  90.7 73.2 %all_to_all.71 = bf16[5,32,128,128]{3,2,0,1:T(8,128)(2,1)} all-to-all(bf16[5,32,128,128]{3,2,0,1:T(8,128)(2,1)} %get-tuple-element.89), channel_id=1, replica_groups=mesh['seq'=32,'head'=4] {'seq'}, dimensions={1} | all-to-all | bytes 10485760 | tf_op jit(solution)/shard_map/all_to_all | solution.py:75
  163.8 5.0 %all-to-all-start.4 = ((bf16[5,32,128,128]{3,2,0,1:T(8,128)(2,1)}), bf16[5,32,128,128]{3,2,0,1:T(8,128)(2,1)}, u32[]{:S(2)}, u32[]{:S(2)}) async-start(bf16[5,32,128,128]{3,2,0,1:T(8,128)(2,1)} %get-tuple-element.88), calls=%async_computation.4 | async-start | bytes 10485760 | tf_op jit(solution)/shard_map/all_to_all | solution.py:76
  174.1 3.2 copy.51
  177.3 4.6 %reshape.121 = f32[2,4,128,5,128]{2,1,0,4,3:T(4,128)} reshape(f32[4,256,640]{1,0,2:T(4,128)} %copy.51) | data formatting | bytes 5242880 | tf_op jit(solution)/shard_map/convert_element_type | solution.py:47
  184.2 3.1 pad_maximum_fusion
  187.2 4.1 %copy.61 = bf16[5,40,128,128]{3,2,1,0:T(8,128)(2,1)} copy(bf16[5,40,128,128]{3,2,0,1:T(8,128)(2,1)S(1)} %pad_maximum_fusion) | data formatting | bytes 13107200 | tf_op jit(solution)/shard_map/while | solution.py:98
  191.3 39.0 %all-to-all-done.4 = bf16[5,32,128,128]{3,2,0,1:T(8,128)(2,1)} async-done(((bf16[5,32,128,128]{3,2,0,1:T(8,128)(2,1)}), bf16[5,32,128,128]{3,2,0,1:T(8,128)(2,1)}, u32[]{:S(2)}, u32[]{:S(2)}) %all-to-all-start.4) | async-done | bytes 5242912 | tf_op jit(solution)/shard_map/all_to_all | solution.py:76
  230.3 3.1 pad_maximum_fusion.1
  233.4 4.2 %copy.62 = bf16[5,40,128,128]{3,2,1,0:T(8,128)(2,1)} copy(bf16[5,40,128,128]{3,2,0,1:T(8,128)(2,1)S(1)} %pad_maximum_fusion.1) | data formatting | bytes 13107200 | tf_op jit(solution)/shard_map/while | solution.py:98
  237.6 125.0 %while.10 = (s32[]{:T(128)}, bf16[2,5,4,128,128]{4,3,2,1,0:T(8,128)(2,1)}, pred[2,4,18,128]{3,2,1,0:T(8,128)(4,1)S(1)}, bf16[2,5,4,128,128]{3,2,0,4,1:T(4,128)(2...) while((s32[]{:T(128)}, ...), condition=%wide.region_9.12_spmd, body=%wide.region_6.11_spmd.sunk | while | flops 3109024256 | bytes 156082960 | solution.py:98
  237.7 9.6 %gather_fusion.1 = bf16[72,5,128,128]{3,2,1,0:T(8,128)(2,1)} fusion(bf16[5,40,128,128]{3,2,1,0:T(8,128)(2,1)} %get-tuple-element.162, s32[1024]{0:T(1024)S(1)} %pad_clamp_fusion.4), kind=kCustom, calls=%fused_computation.1.clone.clone.1 | custom fusion | bytes 23593248 | tf_op jit(solution)/shard_map/while/body/eval_jaxpr/jit(_take)/gather | solution.py:94
  248.4 14.4 %fusion.43 = (f32[5,4,128]{2,1,0:T(4,128)S(1)}, f32[5,4,128,18,128]{2,4,3,1,0:T(8,128)}) fusion(pred[4,18,128]{2,1,0:T(8,128)(4,1)S(1)} %dynamic-slice_bitcast_fusion.4, bf16[4,18,5,128,128]{4,3,2,1,0:T(8,128)(2,1)} %bitcast.105, pred[4,18]{1,0:T(4,128)(4,1)S(1)} %get-tuple-element.138, bf16[1,5,4,128,128]{4,3,2,1,0:T(8,128)(2,1)S(1)} %copy.97), kind=kOutput, calls=%fused_computation.8.clone.1 | convolution fusion | flops 1533539840 | bytes 36064328 | tf_op jit(solution)/shard_map/while/body/eval_jaxpr/hqad,hqkbd->hqakb/dot_general | solution.py:20
  262.8 10.8 %convert_reduce_fusion.2 = f32[5,4,128]{2,1,0:T(4,128)S(1)} fusion(f32[5,4,128]{2,1,0:T(4,128)S(1)} %get-tuple-element.139, f32[5,4,128,18,128]{2,4,3,1,0:T(8,128)} %get-tuple-element.140, pred[4,18,128]{2,1,0:T(8,128)(4,1)S(1)} %dynamic-slice_bitcast_fusion.4), kind=kLoop, calls=%fused_computation.5.clone.1 | loop fusion | flops 35386880 | bytes 23622656 | tf_op jit(solution)/shard_map/while/body/eval_jaxpr/reduce_sum | solution.py:26
  273.6 9.7 %gather_fusion = bf16[72,5,128,128]{3,2,1,0:T(8,128)(2,1)} fusion(bf16[5,40,128,128]{3,2,1,0:T(8,128)(2,1)} %get-tuple-element.163, s32[1024]{0:T(1024)S(1)} %pad_clamp_fusion.4), kind=kCustom, calls=%fused_computation.3.clone.clone.1 | custom fusion | bytes 23593248 | tf_op jit(solution)/shard_map/while/body/eval_jaxpr/jit(_take)/gather | solution.py:95
  283.4 15.7 %fusion.44 = bf16[2,5,4,128,128]{4,3,2,1,0:T(8,128)(2,1)S(1)} fusion(bf16[2,5,4,128,128]{4,3,2,1,0:T(8,128)(2,1)S(1)} %copy-done.10, s32[]{:T(128)} %get-tuple-element.149, bf16[4,18,5,128,128]{4,3,2,1,0:T(8,128)(2,1)} %bitcast.106, pred[4,18]{1,0:T(4,128)(4,1)S(1)} %get-tuple-element.138, f32[5,4,128]{2,1,0:T(4,128)S(1)} %convert_reduce_fusion.2, ...), kind=kOutput, calls=%fused_computation.22.clone.1 | convolution fusion | flops 1540096000 | bytes 36078084 | tf_op jit(solution)/shard_map/while/body/eval_jaxpr/hqakb,hqkbd->hqad/dot_general | solution.py:27
  300.2 9.6 %gather_fusion.1 = bf16[72,5,128,128]{3,2,1,0:T(8,128)(2,1)} fusion(bf16[5,40,128,128]{3,2,1,0:T(8,128)(2,1)} %get-tuple-element.162, s32[1024]{0:T(1024)S(1)} %pad_clamp_fusion.4), kind=kCustom, calls=%fused_computation.1.clone.clone.1 | custom fusion | bytes 23593248 | tf_op jit(solution)/shard_map/while/body/eval_jaxpr/jit(_take)/gather | solution.py:94
  311.0 14.4 %fusion.43 = (f32[5,4,128]{2,1,0:T(4,128)S(1)}, f32[5,4,128,18,128]{2,4,3,1,0:T(8,128)}) fusion(pred[4,18,128]{2,1,0:T(8,128)(4,1)S(1)} %dynamic-slice_bitcast_fusion.4, bf16[4,18,5,128,128]{4,3,2,1,0:T(8,128)(2,1)} %bitcast.105, pred[4,18]{1,0:T(4,128)(4,1)S(1)} %get-tuple-element.138, bf16[1,5,4,128,128]{4,3,2,1,0:T(8,128)(2,1)S(1)} %copy.97), kind=kOutput, calls=%fused_computation.8.clone.1 | convolution fusion | flops 1533539840 | bytes 36064328 | tf_op jit(solution)/shard_map/while/body/eval_jaxpr/hqad,hqkbd->hqakb/dot_general | solution.py:20
  325.3 10.8 %convert_reduce_fusion.2 = f32[5,4,128]{2,1,0:T(4,128)S(1)} fusion(f32[5,4,128]{2,1,0:T(4,128)S(1)} %get-tuple-element.139, f32[5,4,128,18,128]{2,4,3,1,0:T(8,128)} %get-tuple-element.140, pred[4,18,128]{2,1,0:T(8,128)(4,1)S(1)} %dynamic-slice_bitcast_fusion.4), kind=kLoop, calls=%fused_computation.5.clone.1 | loop fusion | flops 35386880 | bytes 23622656 | tf_op jit(solution)/shard_map/while/body/eval_jaxpr/reduce_sum | solution.py:26
  336.1 9.7 %gather_fusion = bf16[72,5,128,128]{3,2,1,0:T(8,128)(2,1)} fusion(bf16[5,40,128,128]{3,2,1,0:T(8,128)(2,1)} %get-tuple-element.163, s32[1024]{0:T(1024)S(1)} %pad_clamp_fusion.4), kind=kCustom, calls=%fused_computation.3.clone.clone.1 | custom fusion | bytes 23593248 | tf_op jit(solution)/shard_map/while/body/eval_jaxpr/jit(_take)/gather | solution.py:95
  345.9 15.7 %fusion.44 = bf16[2,5,4,128,128]{4,3,2,1,0:T(8,128)(2,1)S(1)} fusion(bf16[2,5,4,128,128]{4,3,2,1,0:T(8,128)(2,1)S(1)} %copy-done.10, s32[]{:T(128)} %get-tuple-element.149, bf16[4,18,5,128,128]{4,3,2,1,0:T(8,128)(2,1)} %bitcast.106, pred[4,18]{1,0:T(4,128)(4,1)S(1)} %get-tuple-element.138, f32[5,4,128]{2,1,0:T(4,128)S(1)} %convert_reduce_fusion.2, ...), kind=kOutput, calls=%fused_computation.22.clone.1 | convolution fusion | flops 1540096000 | bytes 36078084 | tf_op jit(solution)/shard_map/while/body/eval_jaxpr/hqakb,hqkbd->hqad/dot_general | solution.py:27
  362.6 2.9 copy.63
  366.6 15.7 %all_to_all.72 = bf16[4,256,640]{1,2,0:T(8,128)(2,1)S(1)} all-to-all(bf16[4,256,640]{1,2,0:T(8,128)(2,1)S(1)} %copy.64), channel_id=1, replica_groups=mesh['seq'=32,'head'=4] {'head'}, dimensions={0} | all-to-all | bytes 2621440 | tf_op jit(solution)/shard_map/all_to_all | solution.py:107
  (92 shorter events, 33.7 us)
Async XLA Ops:
  0.0 30.8 %copy-start = (f32[2560]{0:T(1024)S(1)}, f32[2560]{0:T(1024)}, u32[]{:S(2)}) copy-start(f32[2560]{0:T(1024)} %param.18) | copy-start | bytes 30724
  0.0 7.4 %copy-start.9 = (bf16[256,2560]{1,0:T(8,128)(2,1)S(1)}, bf16[256,2560]{1,0:T(8,128)(2,1)}, u32[]{:S(2)}) copy-start(bf16[256,2560]{1,0:T(8,128)(2,1)} %param.15) | copy-start | bytes 3932164
  0.0 28.1 %copy-start.12 = (s32[256,18]{0,1:T(8,128)S(1)}, s32[256,18]{0,1:T(8,128)}, u32[]{:S(2)}) copy-start(s32[256,18]{0,1:T(8,128)} %param.19) | copy-start | bytes 55300
  0.0 28.1 %copy-start.13 = (s32[256]{0:T(256)S(1)}, s32[256]{0:T(256)}, u32[]{:S(2)}) copy-start(s32[256]{0:T(256)} %param.20) | copy-start | bytes 3076
  2.5 21.8 %all-to-all-start = ((bf16[256,4,640]{0,2,1:T(8,128)(2,1)}), bf16[256,4,640]{0,2,1:T(8,128)(2,1)S(1)}, u32[]{:S(2)}, u32[]{:S(2)}) async-start(bf16[256,4,640]{0,2,1:T(8,128)(2,1)} %bitcast.13), calls=%async_computation | async-start | bytes 2621440 | tf_op jit(solution)/shard_map/all_to_all | solution.py:43
  24.4 24.2 %copy-start.6 = (bf16[256,4,640]{0,2,1:T(8,128)(2,1)}, bf16[256,4,640]{0,2,1:T(8,128)(2,1)S(1)}, u32[]{:S(2)}) copy-start(bf16[256,4,640]{0,2,1:T(8,128)(2,1)S(1)} %all-to-all-done) | copy-start | bytes 3932164
  24.4 19.6 %all-to-all-start.1 = ((bf16[256,4,640]{0,2,1:T(8,128)(2,1)}), bf16[256,4,640]{0,2,1:T(8,128)(2,1)S(1)}, u32[]{:S(2)}, u32[]{:S(2)}) async-start(bf16[256,4,640]{0,2,1:T(8,128)(2,1)} %bitcast.110), calls=%async_computation.1 | async-start | bytes 2621440 | tf_op jit(solution)/shard_map/all_to_all | solution.py:44
  44.0 24.7 %all-to-all-start.3 = ((bf16[256,4,640]{0,2,1:T(8,128)(2,1)}), bf16[256,4,640]{0,2,1:T(8,128)(2,1)}, u32[]{:S(2)}, u32[]{:S(2)}) async-start(bf16[256,4,640]{0,2,1:T(8,128)(2,1)} %bitcast.109), calls=%async_computation.3 | async-start | bytes 2621440 | tf_op jit(solution)/shard_map/all_to_all | solution.py:45
  67.5 1.1 copy-start.3
  163.8 5.4 %copy-start.2 = (s32[256]{0:T(256)S(1)}, s32[256]{0:T(256)}, u32[]{:S(2)}) copy-start(s32[256]{0:T(256)} %param.21) | copy-start | bytes 3076
  163.8 8.1 %copy-start.5 = (bf16[8,128,5,128]{1,0,3,2:T(8,128)(2,1)S(1)}, bf16[8,128,5,128]{1,0,3,2:T(8,128)(2,1)}, u32[]{:S(2)}) copy-start(bf16[8,128,5,128]{1,0,3,2:T(8,128)(2,1)} %reshape.120) | copy-start | bytes 3932164
  163.8 66.5 %all-to-all-start.4 = ((bf16[5,32,128,128]{3,2,0,1:T(8,128)(2,1)}), bf16[5,32,128,128]{3,2,0,1:T(8,128)(2,1)}, u32[]{:S(2)}, u32[]{:S(2)}) async-start(bf16[5,32,128,128]{3,2,0,1:T(8,128)(2,1)} %get-tuple-element.88), calls=%async_computation.4 | async-start | bytes 10485760 | tf_op jit(solution)/shard_map/all_to_all | solution.py:76
  168.8 5.1 %copy-start.7 = (bf16[256,4,640]{0,2,1:T(8,128)(2,1)S(1)}, bf16[256,4,640]{0,2,1:T(8,128)(2,1)}, u32[]{:S(2)}) copy-start(bf16[256,4,640]{0,2,1:T(8,128)(2,1)} %copy-done.6) | copy-start | bytes 3932164
  177.3 6.8 %copy-start.4 = (bf16[5,8,128,128]{3,2,0,1:T(8,128)(2,1)S(1)}, bf16[5,8,128,128]{3,2,0,1:T(8,128)(2,1)}, u32[]{:S(2)}) copy-start(bf16[5,8,128,128]{3,2,0,1:T(8,128)(2,1)} %copy-done.3) | copy-start | bytes 3932164
  187.2 43.1 %copy-start.8 = (bf16[8,128,5,128]{3,1,2,0:T(8,128)(2,1)S(1)}, bf16[8,128,5,128]{3,1,2,0:T(8,128)(2,1)}, u32[]{:S(2)}) copy-start(bf16[8,128,5,128]{3,1,2,0:T(8,128)(2,1)} %copy.58) | copy-start | bytes 3932164
  273.6 9.8 %copy-start.10 = (bf16[2,5,4,128,128]{4,3,2,1,0:T(8,128)(2,1)S(1)}, bf16[2,5,4,128,128]{4,3,2,1,0:T(8,128)(2,1)}, u32[]{:S(2)}) copy-start(bf16[2,5,4,128,128]{4,3,2,1,0:T(8,128)(2,1)} %get-tuple-element.150) | copy-start | bytes 3932164 | tf_op jit(solution)/shard_map/while
  299.1 1.1 copy-start.11
  336.1 9.8 %copy-start.10 = (bf16[2,5,4,128,128]{4,3,2,1,0:T(8,128)(2,1)S(1)}, bf16[2,5,4,128,128]{4,3,2,1,0:T(8,128)(2,1)}, u32[]{:S(2)}) copy-start(bf16[2,5,4,128,128]{4,3,2,1,0:T(8,128)(2,1)} %get-tuple-element.150) | copy-start | bytes 3932164 | tf_op jit(solution)/shard_map/while
  361.6 1.1 copy-start.11
  362.6 21.3 %copy-start.1 = (f32[2560]{0:T(1024)S(1)}, f32[2560]{0:T(1024)}, u32[]{:S(2)}) copy-start(f32[2560]{0:T(1024)} %param.18) | copy-start | bytes 30724
where the time goes:
time: 391 us; the launch traced here: 384 us
  blocking collectives  101 us (26%)
  local copies, waits for them, and re-layouts  97.1 us (25%)
  waiting for transfers between devices  67.3 us (17%)
  matrix products  60.1 us (15%)
  other arithmetic  40.6 us (10%)
  starting transfers between devices  17.7 us (5%)
    all_to_all x1, blocking collectives, on_device(): lax.all_to_all(out_k, 'seq', split_axis=1, concat_axis=1, tiled=True)  73.2 us
    all_to_all x1, waiting for transfers between devices, on_device(): lax.all_to_all(out_v, 'seq', split_axis=1, concat_axis=1, tiled=True)  39 us
    dot_general x2, matrix products, tile_attention(): jnp.einsum('hqakb,hqkbd->hqad', weights, value_block, preferred_element_t...  31.4 us
    dot_general x2, matrix products, tile_attention(): jnp.einsum('hqad,hqkbd->hqakb', query_block, key_block, preferred_element...  28.8 us
    reduce_sum x2, other arithmetic, tile_attention(): total = jnp.sum(weights.astype(jnp.float32), axis=(3, 4))  21.5 us
    gather x2, local copies, waits for them, and re-layouts, attend(): v_block = jnp.take(bank_v, index_block, axis=1)  19.5 us
    gather x2, local copies, waits for them, and re-layouts, attend(): k_block = jnp.take(bank_k, index_block, axis=1)  19.3 us
    all_to_all x1, blocking collectives, on_device(): lax.all_to_all(mixed, 'head', split_axis=0, concat_axis=1, tiled=True)  15.7 us
  transfers between devices with their start and end apart: 4, of which 3 were waited for; matrix products, arithmetic and copies ran while one was open for 9% of the time, Pallas kernels for 0%

commit v1 on v0

v1 whole, which is shorter than its diff:
```python
import functools
import math

import jax
import jax.numpy as jnp
from jax import lax
from jax.experimental import pallas as pl
from jax.experimental.pallas import tpu as pltpu
from jax.sharding import PartitionSpec as P

HD = 128
TILE = 128
EPS = 1e-06
MASKED = -1e30
MESH = pl.DeviceIdType.MESH
LOG2E = math.log2(math.e)


def row_scale(rows_ref, width):
    groups = width // HD
    total = jnp.zeros((rows_ref.shape[0], TILE, HD), jnp.float32)
    for g in range(groups):
        part = rows_ref[:, :, g * HD : (g + 1) * HD].astype(jnp.float32)
        total = total + part * part
    return lax.rsqrt(jnp.sum(total, axis=-1, keepdims=True) / width + EPS)


def kernel(
    n_seq, n_head, heads_here,
    wanted, listed, counts, valid, q_hbm, k_hbm, v_hbm, gain_q, gain_k,
    o_hbm,
    q_in, k_in, q_stage, k_stage, send, out_stage, *rest,
):
    q_blk = rest[:heads_here]
    k_blk = rest[heads_here : 2 * heads_here]
    v_blk = rest[2 * heads_here : 3 * heads_here]
    bank = rest[3 * heads_here : 4 * heads_here]
    (in_sem, own_sem, a_send, a_recv, b_send, b_recv, o_send, o_recv, o_own) = rest[4 * heads_here :]
    s = lax.axis_index("seq")
    x = lax.axis_index("head")
    own_tiles = q_hbm.shape[0]
    span_tiles = own_tiles * n_head
    width = q_hbm.shape[2]
    slots = listed.shape[1]
    mine = pl.ds(x * own_tiles, own_tiles)

    load_k = pltpu.make_async_copy(k_hbm, k_in, in_sem.at[0])
    load_q = pltpu.make_async_copy(q_hbm, q_in, in_sem.at[1])
    load_k.start()
    load_q.start()

    def columns(head):
        return pl.ds(pl.multiple_of(head * HD, HD), HD)

    own_v = []
    for h in range(heads_here):
        copy = pltpu.make_async_copy(
            v_hbm.at[:, :, columns(x * heads_here + h)], v_blk[h].at[mine], own_sem.at[h]
        )
        copy.start()
        own_v.append(copy)

    barrier = pltpu.get_barrier_semaphore()
    for o in range(1, n_head):
        pl.semaphore_signal(
            barrier, inc=1, device_id=(s, lax.rem(x + o, n_head)), device_id_type=MESH
        )

    @pl.loop(1, n_seq)
    def _(d):
        pl.semaphore_signal(
            barrier, inc=1, device_id=(lax.rem(s + d, n_seq), x), device_id_type=MESH
        )

    load_k.wait()
    k_scale = row_scale(k_in, width)
    pl.semaphore_wait(barrier, n_head + n_seq - 2)

    def to_head(kind, h, o, src, dst):
        return pltpu.make_async_remote_copy(
            src_ref=src,
            dst_ref=dst.at[mine],
            send_sem=a_send.at[kind],
            recv_sem=a_recv.at[kind, h, o - 1],
            device_id=(s, lax.rem(x + o, n_head)),
            device_id_type=MESH,
        )

    def spread(kind, h, rows_in, scale, gain, stage, blocks):
        for o in (2, 1, 3, 0):
            cols = columns(lax.rem(x + o, n_head) * heads_here + h)
            rows = rows_in[:, :, cols].astype(jnp.float32)
            rows = (rows * scale * gain[:, cols][None]).astype(jnp.bfloat16)
            if o == 0:
                blocks[h][mine] = rows
            else:
                stage[o - 1, h] = rows
                to_head(kind, h, o, stage.at[o - 1, h], blocks[h]).start()

    def spread_v(h):
        for o in (2, 1, 3):
            cols = columns(lax.rem(x + o, n_head) * heads_here + h)
            to_head(1, h, o, v_hbm.at[:, :, cols], v_blk[h]).start()

    def arrived(kind, h, blocks):
        for o in range(1, n_head):
            pltpu.make_async_copy(
                blocks[h].at[mine], blocks[h].at[mine], a_recv.at[kind, h, o - 1]
            ).wait()

    def exchange(h):
        arrived(0, h, k_blk)
        arrived(1, h, v_blk)
        own_v[h].wait()

        @pl.loop(0, n_seq - 1)
        def _(d):
            peer = lax.rem(s + d + 1, n_seq)
            tile = wanted[peer]
            send[h, d, 0] = k_blk[h][tile]
            send[h, d, 1] = v_blk[h][tile]
            pltpu.make_async_remote_copy(
                src_ref=send.at[h, d],
                dst_ref=bank[h].at[s],
                send_sem=b_send.at[h],
                recv_sem=b_recv.at[h],
                device_id=(peer, x),
                device_id_type=MESH,
            ).start()

    q_scale = None
    for h in range(heads_here):
        spread(0, h, k_in, k_scale, gain_k, k_stage, k_blk)
        spread_v(h)
        bank[h][s] = jnp.zeros(bank[h].shape[1:], bank[h].dtype)
    load_q.wait()
    q_scale = row_scale(q_in, width) * (HD**-0.5 * LOG2E)
    for h in range(heads_here):
        spread(2, h, q_in, q_scale, gain_q, q_stage, q_blk)
    for h in range(heads_here):
        exchange(h)

    lane = lax.broadcasted_iota(jnp.int32, (1, TILE), 1)

    for h in range(heads_here):
        arrived(2, h, q_blk)
        landed = bank[h].at[pl.ds(0, n_seq - 1)]
        pltpu.make_async_copy(landed, landed, b_recv.at[h]).wait()

        @pl.loop(0, span_tiles)
        def _(step, h=h):
            o = n_head - 1 - step // own_tiles
            part = step % own_tiles
            dest = lax.rem(x + o, n_head)
            i = dest * own_tiles + part
            row = s * span_tiles + i
            count = counts[row]
            mate = i + 1 - 2 * (i % 2)
            keys, vals, bias = [], [], []
            for e in range(slots):
                g = listed[row, e]
                if e < 2:
                    own = i if e == 0 else mate
                    keys.append(k_blk[h][own])
                    vals.append(v_blk[h][own])
                else:
                    owner = g // span_tiles
                    keys.append(bank[h][owner, 0])
                    vals.append(bank[h][owner, 1])
                limit = jnp.where(e < count, valid[g], 0)
                bias.append(jnp.where(lane < limit, 0.0, MASKED))
            scores = lax.dot_general(
                q_blk[h][i], jnp.concatenate(keys, axis=0), (((1,), (1,)), ((), ())),
                preferred_element_type=jnp.float32,
            ) + jnp.concatenate(bias, axis=1)
            peak = jnp.max(scores, axis=1, keepdims=True)
            weights = jnp.exp2(scores - peak)
            total = jnp.sum(weights, axis=1, keepdims=True)
            mixed = jnp.dot(
                weights.astype(jnp.bfloat16), jnp.concatenate(vals, axis=0),
                preferred_element_type=jnp.float32,
            )
            out_stage[h, i] = (mixed / total).astype(jnp.bfloat16)

            @pl.when((part == own_tiles - 1) & (o > 0))
            def _():
                pltpu.make_async_remote_copy(
                    src_ref=out_stage.at[h, pl.ds(dest * own_tiles, own_tiles)],
                    dst_ref=o_hbm.at[:, :, columns(x * heads_here + h)],
                    send_sem=o_send.at[h],
                    recv_sem=o_recv.at[h],
                    device_id=(s, dest),
                    device_id_type=MESH,
                ).start()

        pltpu.make_async_copy(
            out_stage.at[h, mine], o_hbm.at[:, :, columns(x * heads_here + h)], o_own.at[h]
        ).start()

    for kind in range(3):
        pltpu.make_async_copy(k_stage, k_stage, a_send.at[kind]).wait()
    for h in range(heads_here):
        pltpu.make_async_copy(send.at[h], send.at[h], b_send.at[h]).wait()
        pltpu.make_async_copy(
            out_stage.at[h, mine], o_hbm.at[:, :, columns(x * heads_here + h)], o_own.at[h]
        ).wait()
        away = out_stage.at[h, pl.ds(0, span_tiles - own_tiles)]
        pltpu.make_async_copy(away, away, o_send.at[h]).wait()
        pltpu.make_async_copy(away, away, o_recv.at[h]).wait()


def on_device(queries, keys, values, gain_q, gain_k, key_tiles, tile_counts, tile_valid):
    n_head = lax.axis_size("head")
    n_seq = lax.axis_size("seq")
    rows, width = queries.shape
    own_tiles = rows // TILE
    span_tiles = own_tiles * n_head
    heads_here = width // HD // n_head
    slots = key_tiles.shape[1]
    s = lax.axis_index("seq")

    grid = key_tiles.reshape(n_seq, span_tiles, slots)
    used = lax.broadcasted_iota(jnp.int32, grid.shape, 2) < tile_counts.reshape(n_seq, span_tiles, 1)
    match = used & (grid // span_tiles == s)
    wanted = jnp.max(jnp.where(match, grid % span_tiles, 0), axis=(1, 2))

    smem = pl.BlockSpec(memory_space=pltpu.SMEM)
    vmem = pl.BlockSpec(memory_space=pltpu.VMEM)
    hbm = pl.BlockSpec(memory_space=pl.ANY)
    bf16 = jnp.bfloat16
    block = pltpu.VMEM((span_tiles, TILE, HD), bf16)
    stage = pltpu.VMEM((n_head - 1, heads_here, own_tiles, TILE, HD), bf16)
    shape = (own_tiles, TILE, width)
    dma = pltpu.SemaphoreType.DMA
    out = pl.pallas_call(
        functools.partial(kernel, n_seq, n_head, heads_here),
        out_shape=jax.ShapeDtypeStruct(shape, bf16),
        in_specs=[smem] * 4 + [hbm] * 3 + [vmem] * 2,
        out_specs=hbm,
        scratch_shapes=[
            pltpu.VMEM(shape, bf16),
            pltpu.VMEM(shape, bf16),
            stage,
            stage,
            pltpu.VMEM((heads_here, n_seq - 1, 2, TILE, HD), bf16),
            pltpu.VMEM((heads_here, span_tiles, TILE, HD), bf16),
            *[block] * (3 * heads_here),
            *[pltpu.VMEM((n_seq, 2, TILE, HD), bf16)] * heads_here,
            dma((2,)),
            dma((heads_here,)),
            dma((3,)),
            dma((3, heads_here, n_head - 1)),
            dma((heads_here,)),
            dma((heads_here,)),
            dma((heads_here,)),
            dma((heads_here,)),
            dma((heads_here,)),
        ],
        compiler_params=pltpu.CompilerParams(
            collective_id=0, has_side_effects=True, vmem_limit_bytes=56 << 20
        ),
    )(
        wanted, key_tiles, tile_counts, tile_valid,
        queries.reshape(shape), keys.reshape(shape), values.reshape(shape),
        gain_q.reshape(1, width), gain_k.reshape(1, width),
    )
    return out.reshape(rows, width)


def solution(mesh):
    placed = P(("seq", "head"), None)
    return jax.shard_map(
        on_device,
        mesh=mesh,
        in_specs=(placed, placed, placed, P(), P(), P(), P(), P()),
        out_specs=placed,
        check_vma=False,
    )
```

time: 391 us -> 162 us (0.41); the launches traced: 384 us -> 162 us
  Pallas kernels: 0 us -> 154 us
  blocking collectives: 101 us -> 0 us
  local copies, waits for them, and re-layouts: 97.1 us -> 6.66 us
  waiting for transfers between devices: 67.3 us -> 0 us
  matrix products: 60.1 us -> 0 us
  other arithmetic: 40.6 us -> 1.49 us
  starting transfers between devices: 17.7 us -> 0 us
    pallas_call x0 -> x1, Pallas kernels: none -> 154 us  [on_device(): pl.pallas_call(functools.partial(kernel, n_seq, n_head, heads_here), out_...]
    all_to_all x2 -> x0, blocking collectives: 88.9 us -> none  [the longest x1 73.2 us: on_device(): lax.all_to_all(out_k, 'seq', split_axis=1, concat_axis=1, tiled=True)]
    all_to_all x4 -> x0, waiting for transfers between devices: 67.3 us -> none  [the longest x1 39 us: on_device(): lax.all_to_all(out_v, 'seq', split_axis=1, concat_axis=1, tiled=True)]
    dot_general x4 -> x0, matrix products: 60.1 us -> none  [the longest x2 31.4 us: tile_attention(): jnp.einsum('hqakb,hqkbd->hqad', weights, value_block, preferred_element_t...]
    gather x8 -> x0, local copies, waits for them, and re-layouts: 47.6 us -> none  [the longest x2 19.5 us: attend(): v_block = jnp.take(bank_v, index_block, axis=1)]
    reduce_sum x4 -> x0, other arithmetic: 22.1 us -> none  [the longest x2 21.5 us: tile_attention(): total = jnp.sum(weights.astype(jnp.float32), axis=(3, 4))]
    all_to_all x4 -> x0, starting transfers between devices: 17.7 us -> none  [the longest x1 5 us: on_device(): lax.all_to_all(out_v, 'seq', split_axis=1, concat_axis=1, tiled=True)]
    convert_element_type x5 -> x0, local copies, waits for them, and re-layouts: 14.2 us -> none  [the longest x2 7.81 us: on_device(): q_float = q_raw.astype(jnp.float32)]
  transfers between devices with their start and end apart: 4 -> 0, of which waited for: 3 -> 0; matrix products, arithmetic and copies ran while one was open for 9% -> 0% of each run, Pallas kernels for 0% -> 0%
where the time goes in v1:
time: 162 us
  Pallas kernels  154 us (95%)
  local copies, waits for them, and re-layouts  6.66 us (4%)
    pallas_call x1, Pallas kernels, on_device(): pl.pallas_call(functools.partial(kernel, n_seq, n_head, heads_here), out_...  154 us
    unnamed x2, local copies, waits for them, and re-layouts  3.96 us

profile of v1, /device:TPU:1, one launch (start us, length us, event | category | flops | bytes accessed | tf_op | source)
XLA Modules:
  0.0 162.0 jit_solution(8422024816085664113)
XLA Ops:
  0.0 0.8 fusion.2
  0.8 1.3 reshape.28.gain_q
  2.1 1.3 reshape.29.gain_k
  3.4 0.1 reduce_max.14
  3.5 0.7 reduce_max.18.wanted
  4.2 1.5 copy.10.listed
  5.7 153.9 %shard_map.82 = bf16[2,128,2560]{2,1,0:T(8,128)(2,1)} custom-call(s32[32]{0:T(128)} %reduce_max.18.wanted, s32[256,18]{1,0:T(8,128)} %copy.10.listed, s32[256]{0:T(256)} %counts.1, s32[256]{0:T(256)} %valid.1, bf16[2,128,2560]{2,1,0:T(8,128)(2,1)} %bitcast.5, bf16[2,128,2560]{2,1,0:T(8,128)(2,1)} %bitcast.6, bf16[2,128,2560]{2,1,0:T(8,128)(2,1)} %bitcast.7, ...), custom_call_target="tpu_custom_call" | custom-call | tf_op jit(solution)/shard_map/pallas_call | solution.py:235
  159.6 2.5 %copy.12 = bf16[256,2560]{1,0:T(8,128)(2,1)} copy(bf16[256,2560]{1,0:T(8,128)(2,1)} %bitcast.4) | data formatting | bytes 2621440

commit v2 on v1

v2 whole, which is shorter than its diff:
```python
import functools
import math

import jax
import jax.numpy as jnp
from jax import lax
from jax.experimental import pallas as pl
from jax.experimental.pallas import tpu as pltpu
from jax.sharding import PartitionSpec as P

HD = 128
TILE = 128
EPS = 1e-06
MASKED = -1e30
MESH = pl.DeviceIdType.MESH
LOG2E = math.log2(math.e)
SIDE = 4
CORES = 2
STRIDE = (SIDE * CORES, CORES)
HOPS = ((2, 0), (2, 1), (1, 0), (3, 0), (1, 1), (3, 1), (0, 1))
PIECE = 2


def schedule(heads):
    steps = [("spread", 0), ("spread", 1), ("scale_q", 0), ("ring", 0), ("spread_q", 0)]
    for t in range(1, heads + 3):
        steps += [("ring", t), ("spread", t + 1), ("relay", t - 1), ("pick", t - 1), ("spread_q", t), ("attend", t - 2)]
    return [(name, h) for name, h in steps if 0 <= h < heads]


def row_scale(rows_ref, width):
    groups = width // HD
    total = jnp.zeros((rows_ref.shape[0], TILE, HD), jnp.float32)
    for g in range(groups):
        part = rows_ref[:, :, g * HD : (g + 1) * HD].astype(jnp.float32)
        total = total + part * part
    return lax.rsqrt(jnp.sum(total, axis=-1, keepdims=True) / width + EPS)


def kernel(
    n_head, heads,
    wanted, listed, counts, valid, q_hbm, k_hbm, v_hbm, gain_q, gain_k,
    o_hbm,
    q_in, k_in, q_stage, k_stage, picked, out_stage, *rest,
):
    q_blk = rest[:heads]
    ring = (rest[heads : 2 * heads], rest[2 * heads : 3 * heads])
    bank = (rest[3 * heads : 4 * heads], rest[4 * heads : 5 * heads])
    (in_sem, own_sem, a_send, a_recv, r_send, r_recv, b_send, b_recv, o_send, o_recv, o_own) = rest[5 * heads :]
    s = lax.axis_index("seq")
    x = lax.axis_index("head")
    place = (s // STRIDE[0], s // STRIDE[1] % SIDE)
    core = s % CORES
    own_tiles = q_hbm.shape[0]
    span_tiles = own_tiles * n_head
    half = span_tiles // 2
    width = q_hbm.shape[2]
    slots = listed.shape[1]
    mine = pl.ds(x * own_tiles, own_tiles)
    states = {}

    def device(axis, along, cross, cores):
        moved = [place[0], place[1]]
        moved[axis] = lax.rem(place[axis] + along, SIDE)
        moved[1 - axis] = lax.rem(place[1 - axis] + cross, SIDE)
        return (moved[0] * STRIDE[0] + moved[1] * STRIDE[1] + lax.rem(core + cores, CORES), x)

    def columns(head):
        return pl.ds(pl.multiple_of(head * HD, HD), HD)

    load_k = pltpu.make_async_copy(k_hbm, k_in, in_sem.at[0])
    load_q = pltpu.make_async_copy(q_hbm, q_in, in_sem.at[1])
    load_k.start()
    load_q.start()

    def home(kind, h):
        return ring[kind][h].at[place[kind]] if kind < 2 else q_blk[h]

    own_v = []
    for h in range(heads):
        copy = pltpu.make_async_copy(
            v_hbm.at[:, :, columns(x * heads + h)], home(1, h).at[mine], own_sem.at[h]
        )
        copy.start()
        own_v.append(copy)

    barrier = pltpu.get_barrier_semaphore()
    friends = [(s, lax.rem(x + o, n_head)) for o in range(1, n_head)]
    friends += [device(0, 0, cross, cores) for cross, cores in HOPS]
    friends += [device(1, 0, cross, cores) for cross, cores in HOPS[:-1]]
    for friend in friends:
        pl.semaphore_signal(barrier, inc=1, device_id=friend, device_id_type=MESH)
    load_k.wait()
    states["k"] = row_scale(k_in, width)
    pl.semaphore_wait(barrier, len(friends))

    def to_head(kind, h, o, src):
        pltpu.make_async_remote_copy(
            src_ref=src,
            dst_ref=home(kind, h).at[mine],
            send_sem=a_send.at[kind],
            recv_sem=a_recv.at[kind, h, o - 1],
            device_id=(s, lax.rem(x + o, n_head)),
            device_id_type=MESH,
        ).start()

    def normalise(kind, h, rows_in, scale, gain, stage):
        for o in (2, 1, 3, 0):
            cols = columns(lax.rem(x + o, n_head) * heads + h)
            rows = rows_in[:, :, cols].astype(jnp.float32)
            rows = (rows * scale * gain[:, cols][None]).astype(jnp.bfloat16)
            if o == 0:
                home(kind, h)[mine] = rows
            else:
                stage[o - 1, h] = rows
                to_head(kind, h, o, stage.at[o - 1, h])

    def spread(h):
        normalise(0, h, k_in, states["k"], gain_k, k_stage)
        for o in (2, 1, 3):
            cols = columns(lax.rem(x + o, n_head) * heads + h)
            to_head(1, h, o, v_hbm.at[:, :, cols])

    def scale_q(h):
        load_q.wait()
        states["q"] = row_scale(q_in, width) * (HD**-0.5 * LOG2E)

    def spread_q(h):
        normalise(2, h, q_in, states["q"], gain_q, q_stage)

    def arrived(kind, h):
        for o in range(1, n_head):
            ref = home(kind, h).at[mine]
            pltpu.make_async_copy(ref, ref, a_recv.at[kind, h, o - 1]).wait()

    def ring_copy(kind, h, slot, tiles, along, sem):
        ref = ring[kind][h].at[slot, tiles]
        return pltpu.make_async_remote_copy(
            src_ref=ref,
            dst_ref=ref,
            send_sem=r_send.at[kind, h],
            recv_sem=r_recv.at[kind, h, sem],
            device_id=device(kind, along, 0, 0),
            device_id_type=MESH,
        )

    def ring_wait(kind, h, tiles, sem):
        ref = ring[kind][h].at[0, pl.ds(0, tiles)]
        pltpu.make_async_copy(ref, ref, r_recv.at[kind, h, sem]).wait()

    def ring_send(h):
        arrived(0, h)
        arrived(1, h)
        own_v[h].wait()
        for first in range(0, span_tiles, PIECE):
            for kind in (0, 1):
                for n, along in enumerate((1, SIDE - 1)):
                    ring_copy(kind, h, place[kind], pl.ds(first, PIECE), along, n).start()

    def relay(h):
        for kind in (0, 1):
            for n, along in enumerate((1, SIDE - 1)):
                ring_wait(kind, h, span_tiles, n)
        for first in range(0, half, PIECE):
            for kind in (0, 1):
                for n, along in enumerate((1, SIDE - 1)):
                    slot = lax.rem(place[kind] + SIDE - along, SIDE)
                    ring_copy(kind, h, slot, pl.ds(n * half + first, PIECE), along, 2 + n).start()

    def pick(h):
        for kind in (0, 1):
            for n in (0, 1):
                ring_wait(kind, h, half, 2 + n)
        for kind in (0, 1):
            here = place[1 - kind] * CORES + core
            for a in range(SIDE):
                bank[kind][h][here, a] = ring[kind][h][a, wanted[(kind * SIDE * CORES + here) * SIDE + a]]
        for n, (cross, cores) in enumerate(HOPS):
            for kind in (0, 1):
                row = lax.rem(place[1 - kind] + cross, SIDE) * CORES + lax.rem(core + cores, CORES)
                for a in range(SIDE):
                    tile = wanted[(kind * SIDE * CORES + row) * SIDE + a]
                    picked[kind, h, n, a] = ring[kind][h][a, tile]
                    if a % PIECE == PIECE - 1:
                        part = pl.ds(a + 1 - PIECE, PIECE)
                        pltpu.make_async_remote_copy(
                            src_ref=picked.at[kind, h, n, part],
                            dst_ref=bank[kind][h].at[place[1 - kind] * CORES + core, part],
                            send_sem=b_send.at[kind, h],
                            recv_sem=b_recv.at[kind, h],
                            device_id=device(kind, 0, cross, cores),
                            device_id_type=MESH,
                        ).start()

    lane = lax.broadcasted_iota(jnp.int32, (1, TILE), 1)

    def attend(h):
        arrived(2, h)
        for kind in (0, 1):
            landed = bank[kind][h].at[pl.ds(0, len(HOPS))]
            pltpu.make_async_copy(landed, landed, b_recv.at[kind, h]).wait()

        @pl.loop(0, span_tiles)
        def _(step):
            o = n_head - 1 - step // own_tiles
            part = step % own_tiles
            dest = lax.rem(x + o, n_head)
            i = dest * own_tiles + part
            row = s * span_tiles + i
            count = counts[row]
            mate = i + 1 - 2 * (i % 2)
            keys, vals, bias = [], [], []
            for e in range(slots):
                g = listed[row, e]
                if e < 2:
                    own = i if e == 0 else mate
                    keys.append(ring[0][h][place[0], own])
                    vals.append(ring[1][h][place[1], own])
                else:
                    owner = g // span_tiles
                    z, y, c = owner // STRIDE[0], owner // STRIDE[1] % SIDE, owner % CORES
                    keys.append(bank[0][h][y * CORES + c, z])
                    vals.append(bank[1][h][z * CORES + c, y])
                limit = jnp.where(e < count, valid[g], 0)
                bias.append(jnp.where(lane < limit, 0.0, MASKED))
            scores = lax.dot_general(
                q_blk[h][i], jnp.concatenate(keys, axis=0), (((1,), (1,)), ((), ())),
                preferred_element_type=jnp.float32,
            ) + jnp.concatenate(bias, axis=1)
            peak = jnp.max(scores, axis=1, keepdims=True)
            weights = jnp.exp2(scores - peak)
            total = jnp.sum(weights, axis=1, keepdims=True)
            mixed = jnp.dot(
                weights.astype(jnp.bfloat16), jnp.concatenate(vals, axis=0),
                preferred_element_type=jnp.float32,
            )
            out_stage[h, i] = (mixed / total).astype(jnp.bfloat16)

            @pl.when((part == own_tiles - 1) & (o > 0))
            def _():
                pltpu.make_async_remote_copy(
                    src_ref=out_stage.at[h, pl.ds(dest * own_tiles, own_tiles)],
                    dst_ref=o_hbm.at[:, :, columns(x * heads + h)],
                    send_sem=o_send.at[h],
                    recv_sem=o_recv.at[h],
                    device_id=(s, dest),
                    device_id_type=MESH,
                ).start()

        pltpu.make_async_copy(
            out_stage.at[h, mine], o_hbm.at[:, :, columns(x * heads + h)], o_own.at[h]
        ).start()

    stages = dict(
        spread=spread, scale_q=scale_q, spread_q=spread_q,
        ring=ring_send, relay=relay, pick=pick, attend=attend,
    )
    for name, h in schedule(heads):
        stages[name](h)

    for kind in range(3):
        pltpu.make_async_copy(k_stage, k_stage, a_send.at[kind]).wait()
    for h in range(heads):
        for kind in (0, 1):
            sent = ring[kind][h].at[pl.ds(0, 3)]
            pltpu.make_async_copy(sent, sent, r_send.at[kind, h]).wait()
            sent = picked.at[kind, h]
            pltpu.make_async_copy(sent, sent, b_send.at[kind, h]).wait()
        pltpu.make_async_copy(
            out_stage.at[h, mine], o_hbm.at[:, :, columns(x * heads + h)], o_own.at[h]
        ).wait()
        away = out_stage.at[h, pl.ds(0, span_tiles - own_tiles)]
        pltpu.make_async_copy(away, away, o_send.at[h]).wait()
        pltpu.make_async_copy(away, away, o_recv.at[h]).wait()


def wanted_tiles(grid, used, s):
    z, y, core = s // STRIDE[0], s // STRIDE[1] % SIDE, s % CORES
    slots = grid.shape[1] * grid.shape[2]
    tiles = jnp.where(used, grid, -1).reshape(SIDE, SIDE, CORES, slots)
    along_y = lax.dynamic_index_in_dim(tiles, z, 0, False).reshape(SIDE * CORES, 1, slots)
    along_z = lax.dynamic_index_in_dim(tiles, y, 1, False).reshape(SIDE * CORES, 1, slots)
    span = jnp.arange(SIDE, dtype=jnp.int32)[None, :, None]
    from_z = span * STRIDE[0] + y * STRIDE[1] + core
    from_y = z * STRIDE[0] + span * STRIDE[1] + core
    tile_count = grid.shape[1]
    found = [
        jnp.max(jnp.where((rows // tile_count == owner) & (rows >= 0), rows % tile_count, 0), axis=2)
        for rows, owner in ((along_y, from_z), (along_z, from_y))
    ]
    return jnp.stack(found).reshape(-1)


def on_device(queries, keys, values, gain_q, gain_k, key_tiles, tile_counts, tile_valid):
    n_head = lax.axis_size("head")
    n_seq = lax.axis_size("seq")
    rows, width = queries.shape
    own_tiles = rows // TILE
    span_tiles = own_tiles * n_head
    heads = width // HD // n_head
    slots = key_tiles.shape[1]
    s = lax.axis_index("seq")

    grid = key_tiles.reshape(n_seq, span_tiles, slots)
    used = lax.broadcasted_iota(jnp.int32, grid.shape, 2) < tile_counts.reshape(n_seq, span_tiles, 1)
    wanted = wanted_tiles(grid, used, s)

    smem = pl.BlockSpec(memory_space=pltpu.SMEM)
    vmem = pl.BlockSpec(memory_space=pltpu.VMEM)
    hbm = pl.BlockSpec(memory_space=pl.ANY)
    bf16 = jnp.bfloat16
    stage = pltpu.VMEM((n_head - 1, heads, own_tiles, TILE, HD), bf16)
    shape = (own_tiles, TILE, width)
    dma = pltpu.SemaphoreType.DMA
    out = pl.pallas_call(
        functools.partial(kernel, n_head, heads),
        out_shape=jax.ShapeDtypeStruct(shape, bf16),
        in_specs=[smem] * 4 + [hbm] * 3 + [vmem] * 2,
        out_specs=hbm,
        scratch_shapes=[
            pltpu.VMEM(shape, bf16),
            pltpu.VMEM(shape, bf16),
            stage,
            stage,
            pltpu.VMEM((2, heads, len(HOPS), SIDE, TILE, HD), bf16),
            pltpu.VMEM((heads, span_tiles, TILE, HD), bf16),
            *[pltpu.VMEM((span_tiles, TILE, HD), bf16)] * heads,
            *[pltpu.VMEM((SIDE, span_tiles, TILE, HD), bf16)] * (2 * heads),
            *[pltpu.VMEM((SIDE * CORES, SIDE, TILE, HD), bf16)] * (2 * heads),
            dma((2,)),
            dma((heads,)),
            dma((3,)),
            dma((3, heads, n_head - 1)),
            dma((2, heads)),
            dma((2, heads, 4)),
            dma((2, heads)),
            dma((2, heads)),
            dma((heads,)),
            dma((heads,)),
            dma((heads,)),
        ],
        compiler_params=pltpu.CompilerParams(
            collective_id=0, has_side_effects=True, vmem_limit_bytes=56 << 20
        ),
    )(
        wanted, key_tiles, tile_counts, tile_valid,
        queries.reshape(shape), keys.reshape(shape), values.reshape(shape),
        gain_q.reshape(1, width), gain_k.reshape(1, width),
    )
    return out.reshape(rows, width)


def solution(mesh):
    placed = P(("seq", "head"), None)
    return jax.shard_map(
        on_device,
        mesh=mesh,
        in_specs=(placed, placed, placed, P(), P(), P(), P(), P()),
        out_specs=placed,
        check_vma=False,
    )
```

time: 162 us -> 149 us (0.920)
  Pallas kernels: 154 us -> 140 us
    pallas_call x1, Pallas kernels: 154 us -> 140 us  [on_device(): pl.pallas_call(functools.partial(kernel, n_head, heads), out_shape=jax.Sh...]
    unnamed x2 -> x4, local copies, waits for them, and re-layouts: 3.96 us -> 3.31 us
where the time goes in v2:
time: 149 us
  Pallas kernels  140 us (94%)
  local copies, waits for them, and re-layouts  7.91 us (5%)
    pallas_call x1, Pallas kernels, on_device(): pl.pallas_call(functools.partial(kernel, n_head, heads), out_shape=jax.Sh...  140 us
    unnamed x4, local copies, waits for them, and re-layouts  3.31 us

profile of v2, /device:TPU:1, one launch (start us, length us, event | category | flops | bytes accessed | tf_op | source)
XLA Modules:
  0.0 148.7 jit_solution(3393686329276646853)
XLA Ops:
  0.0 0.1 iota.20
  0.1 1.3 reshape.251.gain_q
  1.4 1.3 reshape.252.gain_k
  2.7 0.8 lt.41
  3.5 0.1 lt.42
  3.6 0.1 lt.43
  3.7 0.8 copy.14.listed
  4.6 0.0 copy-start
  4.6 0.1 reshape.244
  4.8 0.2 select_reduce_fusion.1
  5.1 0.2 select_reduce_fusion
  5.3 0.1 copy.15
  5.4 0.7 reshape.247.wanted
  6.1 0.0 copy-done
  6.1 140.2 %shard_map.82 = bf16[2,128,2560]{2,1,0:T(8,128)(2,1)} custom-call(s32[64]{0:T(128)} %reshape.247.wanted, s32[256,18]{1,0:T(8,128)} %copy-done, s32[256]{0:T(256)} %counts.1, s32[256]{0:T(256)} %valid.1, bf16[2,128,2560]{2,1,0:T(8,128)(2,1)} %bitcast.7, bf16[2,128,2560]{2,1,0:T(8,128)(2,1)} %bitcast.8, bf16[2,128,2560]{2,1,0:T(8,128)(2,1)} %bitcast.9, ...), custom_call_target="tpu_custom_call" | custom-call | tf_op jit(solution)/shard_map/pallas_call | solution.py:315
  146.2 2.5 %copy.18 = bf16[256,2560]{1,0:T(8,128)(2,1)} copy(bf16[256,2560]{1,0:T(8,128)(2,1)} %bitcast.6) | data formatting | bytes 2621440
  (12 shorter events, 0.1 us)
Async XLA Ops:
  4.6 1.5 %copy-start = (s32[256,18]{1,0:T(8,128)}, s32[256,18]{1,0:T(8,128)S(1)}, u32[]{:S(2)}) copy-start(s32[256,18]{1,0:T(8,128)S(1)} %copy.14.listed) | copy-start | bytes 55300

commit v3 on v2

--- a/solution.py
+++ b/solution.py
@@ -18,13 +18,18 @@
 CORES = 2
 STRIDE = (SIDE * CORES, CORES)
 HOPS = ((2, 0), (2, 1), (1, 0), (3, 0), (1, 1), (3, 1), (0, 1))
-PIECE = 2
+EARLY = 4
 
 
 def schedule(heads):
-    steps = [("spread", 0), ("spread", 1), ("scale_q", 0), ("ring", 0), ("spread_q", 0)]
-    for t in range(1, heads + 3):
-        steps += [("ring", t), ("spread", t + 1), ("relay", t - 1), ("pick", t - 1), ("spread_q", t), ("attend", t - 2)]
+    steps = [("send_v", 0), ("ring_own_v", 0), ("send_k", 0), ("ring_own_k", 0)]
+    for h in range(1, heads):
+        steps += [("ring_own_v", h), ("ring_own_k", h)]
+    steps += [("spread", 1), ("scale_q", 0), ("spread_q", 0), ("spread", 2)]
+    steps += [("ring_rest", 0), ("ring_rest", 1), ("relay", 0)]
+    for t in range(heads + 1):
+        steps += [("pick_first", t), ("relay", t + 1), ("pick_last", t), ("ring_rest", t + 2)]
+        steps += [("spread", t + 3), ("spread_q", t + 1), ("attend", t - 1)]
     return [(name, h) for name, h in steps if 0 <= h < heads]
 
 
@@ -37,11 +42,28 @@
     return lax.rsqrt(jnp.sum(total, axis=-1, keepdims=True) / width + EPS)
 
 
+def find_wanted(s, place, core, span_tiles, listed_rows, count_row, found):
+    slots, tiles = listed_rows.shape
+    used = lax.broadcasted_iota(jnp.int32, (slots, tiles), 0) < count_row[...][None]
+    listed = jnp.where(used, listed_rows[...], -1)
+    owner = listed >> (span_tiles.bit_length() - 1)
+    tile = listed & (span_tiles - 1)
+    for kind in (0, 1):
+        for a in range(SIDE):
+            source = s + (a - place[kind]) * STRIDE[kind]
+            best = jnp.max(jnp.where(owner == source, tile, 0), axis=0, keepdims=True)
+            found[pl.ds(kind * SIDE + a, 1), :] = best
+    best = found[...]
+    for step in (1, 2, 4):
+        best = jnp.maximum(best, pltpu.roll(best, tiles - step, 1))
+    found[...] = best
+
+
 def kernel(
     n_head, heads,
-    wanted, listed, counts, valid, q_hbm, k_hbm, v_hbm, gain_q, gain_k,
+    listed, counts, valid, q_hbm, k_hbm, v_hbm, gain_q, gain_k, listed_rows, count_row,
     o_hbm,
-    q_in, k_in, q_stage, k_stage, picked, out_stage, *rest,
+    q_in, k_in, q_stage, k_stage, picked, out_stage, found, wanted, *rest,
 ):
     q_blk = rest[:heads]
     ring = (rest[heads : 2 * heads], rest[2 * heads : 3 * heads])
@@ -55,7 +77,7 @@
     span_tiles = own_tiles * n_head
     half = span_tiles // 2
     width = q_hbm.shape[2]
-    slots = listed.shape[1]
+    slots = listed.shape[0]
     mine = pl.ds(x * own_tiles, own_tiles)
     states = {}
 
@@ -90,8 +112,12 @@
     friends += [device(1, 0, cross, cores) for cross, cores in HOPS[:-1]]
     for friend in friends:
         pl.semaphore_signal(barrier, inc=1, device_id=friend, device_id_type=MESH)
+    find_wanted(s, place, core, span_tiles, listed_rows, count_row, found)
+    to_smem = pltpu.make_async_copy(found, wanted, in_sem.at[2])
+    to_smem.start()
     load_k.wait()
     states["k"] = row_scale(k_in, width)
+    to_smem.wait()
     pl.semaphore_wait(barrier, len(friends))
 
     def to_head(kind, h, o, src):
@@ -104,34 +130,46 @@
             device_id_type=MESH,
         ).start()
 
-    def normalise(kind, h, rows_in, scale, gain, stage):
-        for o in (2, 1, 3, 0):
-            cols = columns(lax.rem(x + o, n_head) * heads + h)
-            rows = rows_in[:, :, cols].astype(jnp.float32)
-            rows = (rows * scale * gain[:, cols][None]).astype(jnp.bfloat16)
-            if o == 0:
-                home(kind, h)[mine] = rows
-            else:
-                stage[o - 1, h] = rows
-                to_head(kind, h, o, stage.at[o - 1, h])
-
-    def spread(h):
-        normalise(0, h, k_in, states["k"], gain_k, k_stage)
+    def normalised(rows_in, scale, gain, head):
+        cols = columns(head)
+        return (rows_in[:, :, cols].astype(jnp.float32) * scale * gain[cols][None, None]).astype(jnp.bfloat16)
+
+    def send_normalised(kind, h, rows_in, scale, gain, stage):
+        for o in (2, 1, 3):
+            stage[o - 1, h] = normalised(rows_in, scale, gain, lax.rem(x + o, n_head) * heads + h)
+            to_head(kind, h, o, stage.at[o - 1, h])
+
+    def send_k(h):
+        send_normalised(0, h, k_in, states["k"], gain_k, k_stage)
+
+    def send_v(h):
         for o in (2, 1, 3):
             cols = columns(lax.rem(x + o, n_head) * heads + h)
             to_head(1, h, o, v_hbm.at[:, :, cols])
 
+    def spread(h):
+        send_v(h)
+        send_k(h)
+
+    def ring_own_k(h):
+        home(0, h)[mine] = normalised(k_in, states["k"], gain_k, x * heads + h)
+        ring_piece(0, h, 0)
+
+    def ring_own_v(h):
+        own_v[h].wait()
+        ring_piece(1, h, 0)
+
     def scale_q(h):
         load_q.wait()
         states["q"] = row_scale(q_in, width) * (HD**-0.5 * LOG2E)
 
     def spread_q(h):
-        normalise(2, h, q_in, states["q"], gain_q, q_stage)
-
-    def arrived(kind, h):
-        for o in range(1, n_head):
-            ref = home(kind, h).at[mine]
-            pltpu.make_async_copy(ref, ref, a_recv.at[kind, h, o - 1]).wait()
+        q_blk[h][mine] = normalised(q_in, states["q"], gain_q, x * heads + h)
+        send_normalised(2, h, q_in, states["q"], gain_q, q_stage)
+
+    def arrived(kind, h, o):
+        ref = home(kind, h).at[mine]
+        pltpu.make_async_copy(ref, ref, a_recv.at[kind, h, o - 1]).wait()
 
     def ring_copy(kind, h, slot, tiles, along, sem):
         ref = ring[kind][h].at[slot, tiles]
@@ -148,54 +186,61 @@
         ref = ring[kind][h].at[0, pl.ds(0, tiles)]
         pltpu.make_async_copy(ref, ref, r_recv.at[kind, h, sem]).wait()
 
-    def ring_send(h):
-        arrived(0, h)
-        arrived(1, h)
-        own_v[h].wait()
-        for first in range(0, span_tiles, PIECE):
-            for kind in (0, 1):
-                for n, along in enumerate((1, SIDE - 1)):
-                    ring_copy(kind, h, place[kind], pl.ds(first, PIECE), along, n).start()
+    def ring_piece(kind, h, o):
+        tiles = pl.ds(lax.rem(x + n_head - o, n_head) * own_tiles, own_tiles)
+        for n, along in enumerate((1, SIDE - 1)):
+            ring_copy(kind, h, place[kind], tiles, along, n).start()
+
+    def ring_rest(h):
+        for o in (1, 3, 2):
+            for kind in (1, 0):
+                arrived(kind, h, o)
+                ring_piece(kind, h, o)
 
     def relay(h):
         for kind in (0, 1):
             for n, along in enumerate((1, SIDE - 1)):
                 ring_wait(kind, h, span_tiles, n)
-        for first in range(0, half, PIECE):
+        for kind in (0, 1):
+            for n, along in enumerate((1, SIDE - 1)):
+                slot = lax.rem(place[kind] + SIDE - along, SIDE)
+                ring_copy(kind, h, slot, pl.ds(n * half, half), along, 2 + n).start()
+
+    def pick(h, hops):
+        for n in hops:
+            cross, cores = HOPS[n]
             for kind in (0, 1):
-                for n, along in enumerate((1, SIDE - 1)):
-                    slot = lax.rem(place[kind] + SIDE - along, SIDE)
-                    ring_copy(kind, h, slot, pl.ds(n * half + first, PIECE), along, 2 + n).start()
-
-    def pick(h):
+                dest = device(kind, 0, cross, cores)
+                for a in range(SIDE):
+                    picked[kind, h, n, a] = ring[kind][h][a, wanted[kind * SIDE + a, dest[0] * span_tiles]]
+                pltpu.make_async_remote_copy(
+                    src_ref=picked.at[kind, h, n],
+                    dst_ref=bank[kind][h].at[place[1 - kind] * CORES + core],
+                    send_sem=b_send.at[kind, h],
+                    recv_sem=b_recv.at[kind, h],
+                    device_id=dest,
+                    device_id_type=MESH,
+                ).start()
+
+    def pick_first(h):
         for kind in (0, 1):
             for n in (0, 1):
                 ring_wait(kind, h, half, 2 + n)
-        for kind in (0, 1):
-            here = place[1 - kind] * CORES + core
+        pick(h, range(0, EARLY))
+
+    def pick_last(h):
+        pick(h, range(EARLY, len(HOPS)))
+        for kind in (0, 1):
             for a in range(SIDE):
-                bank[kind][h][here, a] = ring[kind][h][a, wanted[(kind * SIDE * CORES + here) * SIDE + a]]
-        for n, (cross, cores) in enumerate(HOPS):
-            for kind in (0, 1):
-                row = lax.rem(place[1 - kind] + cross, SIDE) * CORES + lax.rem(core + cores, CORES)
-                for a in range(SIDE):
-                    tile = wanted[(kind * SIDE * CORES + row) * SIDE + a]
-                    picked[kind, h, n, a] = ring[kind][h][a, tile]
-                    if a % PIECE == PIECE - 1:
-                        part = pl.ds(a + 1 - PIECE, PIECE)
-                        pltpu.make_async_remote_copy(
-                            src_ref=picked.at[kind, h, n, part],
-                            dst_ref=bank[kind][h].at[place[1 - kind] * CORES + core, part],
-                            send_sem=b_send.at[kind, h],
-                            recv_sem=b_recv.at[kind, h],
-                            device_id=device(kind, 0, cross, cores),
-                            device_id_type=MESH,
-                        ).start()
+                bank[kind][h][place[1 - kind] * CORES + core, a] = ring[kind][h][
+                    a, wanted[kind * SIDE + a, s * span_tiles]
+                ]
 
     lane = lax.broadcasted_iota(jnp.int32, (1, TILE), 1)
 
     def attend(h):
-        arrived(2, h)
+        for o in range(1, n_head):
+            arrived(2, h, o)
         for kind in (0, 1):
             landed = bank[kind][h].at[pl.ds(0, len(HOPS))]
             pltpu.make_async_copy(landed, landed, b_recv.at[kind, h]).wait()
@@ -211,7 +256,7 @@
             mate = i + 1 - 2 * (i % 2)
             keys, vals, bias = [], [], []
             for e in range(slots):
-                g = listed[row, e]
+                g = listed[e, row]
                 if e < 2:
                     own = i if e == 0 else mate
                     keys.append(ring[0][h][place[0], own])
@@ -252,8 +297,9 @@
         ).start()
 
     stages = dict(
-        spread=spread, scale_q=scale_q, spread_q=spread_q,
-        ring=ring_send, relay=relay, pick=pick, attend=attend,
+        send_v=send_v, send_k=send_k, spread=spread, scale_q=scale_q, spread_q=spread_q,
+        ring_own_k=ring_own_k, ring_own_v=ring_own_v, ring_rest=ring_rest,
+        relay=relay, pick_first=pick_first, pick_last=pick_last, attend=attend,
     )
     for name, h in schedule(heads):
         stages[name](h)
@@ -274,37 +320,14 @@
         pltpu.make_async_copy(away, away, o_recv.at[h]).wait()
 
 
-def wanted_tiles(grid, used, s):
-    z, y, core = s // STRIDE[0], s // STRIDE[1] % SIDE, s % CORES
-    slots = grid.shape[1] * grid.shape[2]
-    tiles = jnp.where(used, grid, -1).reshape(SIDE, SIDE, CORES, slots)
-    along_y = lax.dynamic_index_in_dim(tiles, z, 0, False).reshape(SIDE * CORES, 1, slots)
-    along_z = lax.dynamic_index_in_dim(tiles, y, 1, False).reshape(SIDE * CORES, 1, slots)
-    span = jnp.arange(SIDE, dtype=jnp.int32)[None, :, None]
-    from_z = span * STRIDE[0] + y * STRIDE[1] + core
-    from_y = z * STRIDE[0] + span * STRIDE[1] + core
-    tile_count = grid.shape[1]
-    found = [
-        jnp.max(jnp.where((rows // tile_count == owner) & (rows >= 0), rows % tile_count, 0), axis=2)
-        for rows, owner in ((along_y, from_z), (along_z, from_y))
-    ]
-    return jnp.stack(found).reshape(-1)
-
-
 def on_device(queries, keys, values, gain_q, gain_k, key_tiles, tile_counts, tile_valid):
     n_head = lax.axis_size("head")
-    n_seq = lax.axis_size("seq")
     rows, width = queries.shape
     own_tiles = rows // TILE
     span_tiles = own_tiles * n_head
     heads = width // HD // n_head
-    slots = key_tiles.shape[1]
-    s = lax.axis_index("seq")
-
-    grid = key_tiles.reshape(n_seq, span_tiles, slots)
-    used = lax.broadcasted_iota(jnp.int32, grid.shape, 2) < tile_counts.reshape(n_seq, span_tiles, 1)
-    wanted = wanted_tiles(grid, used, s)
-
+    tiles = key_tiles.shape[0]
+    listed = key_tiles.T
     smem = pl.BlockSpec(memory_space=pltpu.SMEM)
     vmem = pl.BlockSpec(memory_space=pltpu.VMEM)
     hbm = pl.BlockSpec(memory_space=pl.ANY)
@@ -315,7 +338,7 @@
     out = pl.pallas_call(
         functools.partial(kernel, n_head, heads),
         out_shape=jax.ShapeDtypeStruct(shape, bf16),
-        in_specs=[smem] * 4 + [hbm] * 3 + [vmem] * 2,
+        in_specs=[smem] * 3 + [hbm] * 3 + [vmem] * 4,
         out_specs=hbm,
         scratch_shapes=[
             pltpu.VMEM(shape, bf16),
@@ -324,10 +347,12 @@
             stage,
             pltpu.VMEM((2, heads, len(HOPS), SIDE, TILE, HD), bf16),
             pltpu.VMEM((heads, span_tiles, TILE, HD), bf16),
+            pltpu.VMEM((2 * SIDE, tiles), jnp.int32),
+            pltpu.SMEM((2 * SIDE, tiles), jnp.int32),
             *[pltpu.VMEM((span_tiles, TILE, HD), bf16)] * heads,
             *[pltpu.VMEM((SIDE, span_tiles, TILE, HD), bf16)] * (2 * heads),
             *[pltpu.VMEM((SIDE * CORES, SIDE, TILE, HD), bf16)] * (2 * heads),
-            dma((2,)),
+            dma((3,)),
             dma((heads,)),
             dma((3,)),
             dma((3, heads, n_head - 1)),
@@ -343,9 +368,9 @@
             collective_id=0, has_side_effects=True, vmem_limit_bytes=56 << 20
         ),
     )(
-        wanted, key_tiles, tile_counts, tile_valid,
+        listed, tile_counts, tile_valid,
         queries.reshape(shape), keys.reshape(shape), values.reshape(shape),
-        gain_q.reshape(1, width), gain_k.reshape(1, width),
+        gain_q, gain_k, listed, tile_counts,
     )
     return out.reshape(rows, width)
 

time: 149 us -> 127 us (0.85)
  Pallas kernels: 140 us -> 124 us
  local copies, waits for them, and re-layouts: 7.91 us -> 2.46 us
    pallas_call x1, Pallas kernels: 140 us -> 124 us  [on_device(): pl.pallas_call(functools.partial(kernel, n_head, heads), out_shape=jax.Sh...]
    reshape x6 -> x0, local copies, waits for them, and re-layouts: 3.43 us -> none  [the longest x1 1.31 us: on_device(): gain_q.reshape(1, width)]
    unnamed x4 -> x1, local copies, waits for them, and re-layouts: 3.31 us -> 2.46 us
where the time goes in v3:
time: 127 us
  Pallas kernels  124 us (98%)
  local copies, waits for them, and re-layouts  2.46 us (2%)
    pallas_call x1, Pallas kernels, on_device(): pl.pallas_call(functools.partial(kernel, n_head, heads), out_shape=jax.Sh...  124 us

profile of v3, /device:TPU:1, one launch (start us, length us, event | category | flops | bytes accessed | tf_op | source)
XLA Modules:
  0.0 126.7 jit_solution(10197202413006395182)
XLA Ops:
  0.0 124.2 %shard_map.82 = bf16[2,128,2560]{2,1,0:T(8,128)(2,1)} custom-call(s32[18,256]{1,0:T(8,128)} %bitcast.9, s32[256]{0:T(256)} %count_row.1, s32[256]{0:T(256)} %valid.1, bf16[2,128,2560]{2,1,0:T(8,128)(2,1)} %bitcast.6, bf16[2,128,2560]{2,1,0:T(8,128)(2,1)} %bitcast.7, bf16[2,128,2560]{2,1,0:T(8,128)(2,1)} %bitcast.8, f32[2560]{0:T(1024)} %gain_q.1, ...), custom_call_target="tpu_custom_call" | custom-call | tf_op jit(solution)/shard_map/pallas_call | solution.py:338
  124.2 2.5 %copy.10 = bf16[256,2560]{1,0:T(8,128)(2,1)} copy(bf16[256,2560]{1,0:T(8,128)(2,1)} %bitcast.5) | data formatting | bytes 2621440

commit v4 on v0

v4 whole, which is shorter than its diff:
```python
import functools
import math

import jax
import jax.numpy as jnp
from jax import lax
from jax.experimental import pallas as pl
from jax.experimental.pallas import tpu as pltpu
from jax.sharding import PartitionSpec as P

HD = 128
TILE = 128
EPS = 1e-06
MASKED = -1e30
MESH = pl.DeviceIdType.MESH
LOG2E = math.log2(math.e)
SIDE = 4
CORES = 2
STRIDE = (SIDE * CORES, CORES)
COLUMNS = SIDE * SIDE
HOPS = ((2, 0), (2, 1), (1, 0), (3, 0), (1, 1), (3, 1), (0, 1))
CHUNKS = (0, 1, 3, 2)
GROUPS = 4
K, V, Q = 0, 1, 2


def schedule():
    return (
        [("send", V), ("scale", K), ("spread_k", 0), ("send", K)]
        + [("own_ring", V), ("own_ring", K), ("direct", K, 0), ("spread_v", 0)]
        + [("direct", K, q) for q in CHUNKS[1:]]
        + [("scale", Q), ("spread_q", 0), ("send", Q)]
        + [("pass_on", K, 0), ("ring_rest", 0), ("direct", V, 0), ("pass_on", K, 1), ("pass_on", K, 3)]
        + [("direct", V, 1), ("pass_on", K, 2), ("finish", K, 0), ("direct", V, 3), ("finish", K, 1)]
        + [("relay", 0), ("direct", V, 2), ("finish", K, 3), ("finish", K, 2), ("pick", 0)]
        + [("complete", K), ("weigh", 0), ("pass_on", V, 0), ("weigh", 1), ("pass_on", V, 1)]
        + [("finish", V, 0), ("attend", 0), ("pass_on", V, 3), ("weigh", 2), ("pass_on", V, 2)]
        + [("finish", V, 1), ("weigh", 3), ("finish", V, 3), ("finish", V, 2)]
        + [("complete", V), ("mix", 0)]
    )


def row_scale(rows_ref, width):
    total = jnp.zeros((rows_ref.shape[0], TILE, HD), jnp.float32)
    for g in range(width // HD):
        part = rows_ref[:, :, g * HD : (g + 1) * HD].astype(jnp.float32)
        total = total + part * part
    return lax.rsqrt(jnp.sum(total, axis=-1, keepdims=True) / width + EPS)


def find_wanted(s, place, span_tiles, listed_rows, count_row, found):
    slots, tiles = listed_rows.shape
    used = lax.broadcasted_iota(jnp.int32, (slots, tiles), 0) < count_row[...][None]
    listed = jnp.where(used, listed_rows[...], -1)
    owner = listed >> (span_tiles.bit_length() - 1)
    tile = listed & (span_tiles - 1)
    for kind in (K, V):
        for a in range(SIDE):
            source = s + (a - place[kind]) * STRIDE[kind]
            best = jnp.max(jnp.where(owner == source, tile, 0), axis=0, keepdims=True)
            found[pl.ds(kind * SIDE + a, 1), :] = best
    best = found[...]
    for step in (1, 2, 4):
        best = jnp.maximum(best, pltpu.roll(best, tiles - step, 1))
    found[...] = best


def kernel(
    n_head,
    listed, counts, valid, q_hbm, k_hbm, v_hbm, gain_q, gain_k, listed_rows, count_row,
    o_ref,
    q_in, k_in, q_norm, k_norm, found, wanted,
    col_k, col_v, col_q, col_out, weights, inverse,
    ring_k, ring_v, bank_k, bank_v, blk_q, picked, blk_out,
    in_sem, own_sem, m_send, m_recv, x_send, x_recv, c_send, c_recv,
    a_send, a_recv, r_send, r_recv, b_send, b_recv, o_send, o_recv, o_own,
):
    s = lax.axis_index("seq")
    x = lax.axis_index("head")
    place = (s // STRIDE[0], s // STRIDE[1] % SIDE)
    core = s % CORES
    here = place[0] * SIDE + place[1]
    own_tiles = q_hbm.shape[0]
    span_tiles = own_tiles * n_head
    half = span_tiles // 2
    width = q_hbm.shape[2]
    slots = listed.shape[0]
    mine = pl.ds(x * own_tiles, own_tiles)
    raw = (k_in, None, q_in)
    norm = (k_norm, None, q_norm)
    gain = (gain_k, None, gain_q)
    col = (col_k, col_v, col_q)
    ring = (ring_k, ring_v)
    bank = (bank_k, bank_v)
    scales = {}

    def device(dz, dy, cores):
        z = lax.rem(place[0] + dz, SIDE)
        y = lax.rem(place[1] + dy, SIDE)
        return (z * STRIDE[0] + y * STRIDE[1] + lax.rem(core + cores, CORES), x)

    def crossing(kind, along, cross, cores):
        return device(along, cross, cores) if kind == K else device(cross, along, cores)

    def beside(o):
        return (s, lax.rem(x + o, n_head))

    def columns(head):
        return pl.ds(pl.multiple_of(head * HD, HD), HD)

    def remote(src, dst, send_sem, recv_sem, dest):
        pltpu.make_async_remote_copy(
            src_ref=src, dst_ref=dst, send_sem=send_sem, recv_sem=recv_sem,
            device_id=dest, device_id_type=MESH,
        ).start()

    def await_bytes(ref, sem):
        pltpu.make_async_copy(ref, ref, sem).wait()

    load_k = pltpu.make_async_copy(k_hbm, k_in, in_sem.at[0])
    load_q = pltpu.make_async_copy(q_hbm, q_in, in_sem.at[1])
    load_k.start()
    load_q.start()
    rest_head = COLUMNS + x
    own_rest = pltpu.make_async_copy(
        v_hbm.at[:, :, columns(rest_head)], ring_v.at[place[1], mine], own_sem.at[0]
    )
    own_col = pltpu.make_async_copy(
        v_hbm.at[:, :, columns(here)], col_v.at[core, x, here], own_sem.at[1]
    )
    own_rest.start()
    own_col.start()

    barrier = pltpu.get_barrier_semaphore()
    friends = [beside(o) for o in range(1, n_head)]
    friends += [device(dz, dy, 0) for dz in range(SIDE) for dy in range(SIDE) if dz + dy]
    friends += [device(0, dy, 1) for dy in range(SIDE)] + [device(dz, 0, 1) for dz in range(1, SIDE)]
    for friend in friends:
        pl.semaphore_signal(barrier, inc=1, device_id=friend, device_id_type=MESH)
    find_wanted(s, place, span_tiles, listed_rows, count_row, found)
    to_smem = pltpu.make_async_copy(found, wanted, in_sem.at[2])
    to_smem.start()
    pl.semaphore_wait(barrier, len(friends))

    def scale(kind):
        (load_k if kind == K else load_q).wait()
        scales[kind] = row_scale(raw[kind], width)
        if kind == Q:
            scales[kind] = scales[kind] * (HD**-0.5 * LOG2E)

    def normalised(kind, head):
        cols = columns(head)
        rows = raw[kind][:, :, cols].astype(jnp.float32)
        return (rows * scales[kind] * gain[kind][cols][None, None]).astype(jnp.bfloat16)

    def source(kind, head):
        if kind == V:
            return v_hbm.at[:, :, columns(head)]
        norm[kind][head] = normalised(kind, head)
        return norm[kind].at[head]

    def to_columns(kind):
        for dz in CHUNKS:
            for dy in CHUNKS:
                if dz + dy:
                    z, y = lax.rem(place[0] + dz, SIDE), lax.rem(place[1] + dy, SIDE)
                    landing = col_q.at[here] if kind == Q else col[kind].at[core, x, here]
                    remote(
                        source(kind, z * SIDE + y), landing, m_send.at[kind],
                        m_recv.at[kind, (SIDE - dz) % SIDE], device(dz, dy, 0),
                    )

    def spread_k(_):
        col_k[core, x, here] = normalised(K, here)
        to_columns(K)

    def spread_v(_):
        to_columns(V)

    def spread_q(_):
        col_q[here] = normalised(Q, here)
        to_columns(Q)

    def chunk_rows(q, first=0, count=SIDE):
        return pl.ds(lax.rem(place[0] + q, SIDE) * SIDE + first, count)

    def chunk_wait(kind, q):
        landed = col_k.at[0, 0, pl.ds(0, SIDE - 1 if q == 0 else SIDE)]
        await_bytes(landed, m_recv.at[kind, q])

    def across(kind, slot, rows):
        ref = col[kind].at[core, slot, rows]
        remote(ref, ref, c_send.at[kind], c_recv.at[kind], device(0, 0, 1))

    def direct(kind, q):
        if kind == V and q == 0:
            own_col.wait()
        chunk_wait(kind, q)
        ref = col[kind].at[core, x, chunk_rows(q)]
        for n, along in enumerate((1, SIDE - 1)):
            remote(ref, ref, x_send.at[kind], x_recv.at[kind, n, q], beside(along))
        across(kind, x, chunk_rows(q))

    def pass_on(kind, q):
        for n, along in enumerate((1, SIDE - 1)):
            slot = lax.rem(x + SIDE - along, SIDE)
            await_bytes(col[kind].at[core, slot, chunk_rows(q)], x_recv.at[kind, n, q])
            ref = col[kind].at[core, slot, chunk_rows(q, n * (SIDE // 2), SIDE // 2)]
            remote(ref, ref, x_send.at[kind], x_recv.at[kind, 2 + n, q], beside(along))
            across(kind, slot, chunk_rows(q))

    def finish(kind, q):
        slot = lax.rem(x + SIDE // 2, SIDE)
        for n in (0, 1):
            ref = col[kind].at[core, slot, chunk_rows(q, n * (SIDE // 2), SIDE // 2)]
            await_bytes(ref, x_recv.at[kind, 2 + n, q])
        across(kind, slot, chunk_rows(q))

    def complete(kind):
        await_bytes(col[kind].at[1 - core], c_recv.at[kind])
        if kind == K:
            for q in CHUNKS:
                chunk_wait(Q, q)

    lane = lax.broadcasted_iota(jnp.int32, (1, TILE), 1)

    def key_bias(row):
        count = counts[row]
        bias = []
        for e in range(slots):
            limit = jnp.where(e < count, valid[listed[e, row]], 0)
            bias.append(jnp.where(lane < limit, 0.0, MASKED))
        return jnp.concatenate(bias, axis=1)

    def softmax(query, keys, bias):
        scores = lax.dot_general(
            query, jnp.concatenate(keys, axis=0), (((1,), (1,)), ((), ())),
            preferred_element_type=jnp.float32,
        ) + bias
        rows = jnp.exp2(scores - jnp.max(scores, axis=1, keepdims=True))
        return rows.astype(jnp.bfloat16), 1.0 / jnp.sum(rows, axis=1, keepdims=True)

    def col_tile(ref, g):
        block = g // span_tiles
        return ref[block % CORES, g % span_tiles // own_tiles, block // CORES, g % own_tiles]

    def col_row(block, part):
        return (block * CORES + core) * span_tiles + x * own_tiles + part

    def weigh(group):
        each = COLUMNS // GROUPS

        @pl.loop(group * each, (group + 1) * each)
        def _(block):
            for part in range(own_tiles):
                row = col_row(block, part)
                keys = [col_tile(col_k, listed[e, row]) for e in range(slots)]
                rows, inv = softmax(col_q[block, part], keys, key_bias(row))
                weights[block, part] = rows
                inverse[block, part] = inv

    def mix(_):
        @pl.loop(0, COLUMNS)
        def _(step):
            off = COLUMNS - 1 - step
            dz, dy = off // SIDE, off % SIDE
            z, y = lax.rem(place[0] + dz, SIDE), lax.rem(place[1] + dy, SIDE)
            block = z * SIDE + y
            for part in range(own_tiles):
                row = col_row(block, part)
                vals = [col_tile(col_v, listed[e, row]) for e in range(slots)]
                mixed = jnp.dot(
                    weights[block, part], jnp.concatenate(vals, axis=0),
                    preferred_element_type=jnp.float32,
                )
                col_out[block, part] = (mixed * inverse[block, part]).astype(jnp.bfloat16)

            @pl.when(off > 0)
            def _():
                remote(
                    col_out.at[block], o_ref.at[:, :, columns(here)], o_send.at[0], o_recv.at[0],
                    (z * STRIDE[0] + y * STRIDE[1] + core, x),
                )

        pltpu.make_async_copy(col_out.at[here], o_ref.at[:, :, columns(here)], o_own.at[0]).start()

    def home(kind):
        return blk_q if kind == Q else ring[kind].at[place[kind]]

    def send(kind):
        for o in (2, 1, 3):
            remote(
                source(kind, COLUMNS + lax.rem(x + o, n_head)), home(kind).at[mine],
                a_send.at[kind], a_recv.at[kind, o - 1], beside(o),
            )
        if kind == Q:
            blk_q[mine] = normalised(Q, rest_head)

    def arrived(kind, o):
        await_bytes(home(kind).at[mine], a_recv.at[kind, o - 1])

    def ring_copy(kind, slot, tiles, n, sem):
        ref = ring[kind].at[slot, tiles]
        along = (1, SIDE - 1)[n]
        remote(ref, ref, r_send.at[kind], r_recv.at[kind, sem], crossing(kind, along, 0, 0))

    def ring_piece(kind, o):
        tiles = pl.ds(lax.rem(x + n_head - o, n_head) * own_tiles, own_tiles)
        for n in (0, 1):
            ring_copy(kind, place[kind], tiles, n, n)

    def own_ring(kind):
        if kind == V:
            own_rest.wait()
        else:
            ring_k[place[K], mine] = normalised(K, rest_head)
        ring_piece(kind, 0)

    def ring_rest(_):
        for o in (1, 3, 2):
            for kind in (V, K):
                arrived(kind, o)
                ring_piece(kind, o)

    def relay(_):
        for kind in (K, V):
            for n in (0, 1):
                await_bytes(ring[kind].at[0], r_recv.at[kind, n])
        for kind in (K, V):
            for n, along in enumerate((1, SIDE - 1)):
                slot = lax.rem(place[kind] + SIDE - along, SIDE)
                ring_copy(kind, slot, pl.ds(n * half, half), n, 2 + n)

    def pick(_):
        to_smem.wait()
        for kind in (K, V):
            for n in (0, 1):
                await_bytes(ring[kind].at[0, pl.ds(0, half)], r_recv.at[kind, 2 + n])
        for n, (cross, cores) in enumerate(HOPS):
            for kind in (K, V):
                dest = crossing(kind, 0, cross, cores)
                for a in range(SIDE):
                    picked[kind, n, a] = ring[kind][a, wanted[kind * SIDE + a, dest[0] * span_tiles]]
                remote(
                    picked.at[kind, n], bank[kind].at[place[1 - kind] * CORES + core],
                    b_send.at[kind], b_recv.at[kind], dest,
                )
        for kind in (K, V):
            for a in range(SIDE):
                bank[kind][place[1 - kind] * CORES + core, a] = ring[kind][
                    a, wanted[kind * SIDE + a, s * span_tiles]
                ]

    def attend(_):
        for o in range(1, n_head):
            arrived(Q, o)
        for kind in (K, V):
            await_bytes(bank[kind].at[pl.ds(0, len(HOPS))], b_recv.at[kind])

        @pl.loop(0, span_tiles)
        def _(step):
            o = n_head - 1 - step // own_tiles
            part = step % own_tiles
            dest = lax.rem(x + o, n_head)
            i = dest * own_tiles + part
            row = s * span_tiles + i
            mate = i + 1 - 2 * (i % 2)
            keys = [ring_k[place[K], i], ring_k[place[K], mate]]
            vals = [ring_v[place[V], i], ring_v[place[V], mate]]
            for e in range(2, slots):
                owner = listed[e, row] // span_tiles
                z, y, c = owner // STRIDE[0], owner // STRIDE[1] % SIDE, owner % CORES
                keys.append(bank_k[y * CORES + c, z])
                vals.append(bank_v[z * CORES + c, y])
            rows, inv = softmax(blk_q[i], keys, key_bias(row))
            mixed = jnp.dot(rows, jnp.concatenate(vals, axis=0), preferred_element_type=jnp.float32)
            blk_out[i] = (mixed * inv).astype(jnp.bfloat16)

            @pl.when((part == own_tiles - 1) & (o > 0))
            def _():
                remote(
                    blk_out.at[pl.ds(dest * own_tiles, own_tiles)], o_ref.at[:, :, columns(rest_head)],
                    o_send.at[1], o_recv.at[1], (s, dest),
                )

        pltpu.make_async_copy(blk_out.at[mine], o_ref.at[:, :, columns(rest_head)], o_own.at[1]).start()

    stages = dict(
        send=send, scale=scale, spread_k=spread_k, spread_v=spread_v, spread_q=spread_q,
        own_ring=own_ring, direct=direct, pass_on=pass_on, finish=finish, complete=complete,
        ring_rest=ring_rest, relay=relay, pick=pick, weigh=weigh, attend=attend, mix=mix,
    )
    for name, *args in schedule():
        stages[name](*args)

    away = col_q.at[pl.ds(0, COLUMNS - 1)]
    aside = blk_q.at[pl.ds(0, span_tiles - own_tiles)]
    for kind in (K, V, Q):
        await_bytes(away, m_send.at[kind])
        await_bytes(aside, a_send.at[kind])
    for kind in (K, V):
        await_bytes(col_k.at[0, pl.ds(0, 3)], x_send.at[kind])
        await_bytes(col_k.at[0], c_send.at[kind])
        await_bytes(ring_k.at[pl.ds(0, 3)], r_send.at[kind])
        await_bytes(picked.at[kind], b_send.at[kind])
    for n, (moved, kept, head) in enumerate(
        ((away, col_out.at[here], here), (aside, blk_out.at[mine], rest_head))
    ):
        await_bytes(moved, o_send.at[n])
        await_bytes(moved, o_recv.at[n])
        pltpu.make_async_copy(kept, o_ref.at[:, :, columns(head)], o_own.at[n]).wait()


def on_device(queries, keys, values, gain_q, gain_k, key_tiles, tile_counts, tile_valid):
    n_head = lax.axis_size("head")
    rows, width = queries.shape
    own_tiles = rows // TILE
    span_tiles = own_tiles * n_head
    heads = width // HD
    tiles, slots = key_tiles.shape
    listed = key_tiles.T

    smem = pl.BlockSpec(memory_space=pltpu.SMEM)
    vmem = pl.BlockSpec(memory_space=pltpu.VMEM)
    hbm = pl.BlockSpec(memory_space=pl.ANY)
    shape = (own_tiles, TILE, width)
    dma = pltpu.SemaphoreType.DMA

    def buffer(*lead, tail=(TILE, HD), kind=jnp.bfloat16):
        return pltpu.VMEM((*lead, *tail), kind)

    out = pl.pallas_call(
        functools.partial(kernel, n_head),
        out_shape=pltpu.VMEM(shape, jnp.bfloat16),
        in_specs=[smem] * 3 + [hbm] * 3 + [vmem] * 4,
        out_specs=hbm,
        scratch_shapes=[
            pltpu.VMEM(shape, jnp.bfloat16),
            pltpu.VMEM(shape, jnp.bfloat16),
            buffer(heads, own_tiles),
            buffer(heads, own_tiles),
            pltpu.VMEM((2 * SIDE, tiles), jnp.int32),
            pltpu.SMEM((2 * SIDE, tiles), jnp.int32),
            buffer(CORES, n_head, COLUMNS, own_tiles),
            buffer(CORES, n_head, COLUMNS, own_tiles),
            buffer(COLUMNS, own_tiles),
            buffer(COLUMNS, own_tiles),
            buffer(COLUMNS, own_tiles, tail=(TILE, slots * TILE)),
            buffer(COLUMNS, own_tiles, tail=(TILE, 1), kind=jnp.float32),
            buffer(SIDE, span_tiles),
            buffer(SIDE, span_tiles),
            buffer(SIDE * CORES, SIDE),
            buffer(SIDE * CORES, SIDE),
            buffer(span_tiles),
            buffer(2, len(HOPS), SIDE),
            buffer(span_tiles),
            dma((3,)),
            dma((2,)),
            dma((3,)),
            dma((3, SIDE)),
            dma((2,)),
            dma((2, 4, SIDE)),
            dma((2,)),
            dma((2,)),
            dma((3,)),
            dma((3, n_head - 1)),
            dma((2,)),
            dma((2, 4)),
            dma((2,)),
            dma((2,)),
            dma((2,)),
            dma((2,)),
            dma((2,)),
        ],
        compiler_params=pltpu.CompilerParams(
            collective_id=0, has_side_effects=True, vmem_limit_bytes=58 << 20
        ),
    )(
        listed, tile_counts, tile_valid,
        queries.reshape(shape), keys.reshape(shape), values.reshape(shape),
        gain_q, gain_k, listed, tile_counts,
    )
    return out.reshape(rows, width)


def solution(mesh):
    placed = P(("seq", "head"), None)
    return jax.shard_map(
        on_device,
        mesh=mesh,
        in_specs=(placed, placed, placed, P(), P(), P(), P(), P()),
        out_specs=placed,
        check_vma=False,
    )
```

time: 391 us -> 122 us (0.31); the launches traced: 384 us -> 122 us
  Pallas kernels: 0 us -> 121 us
  blocking collectives: 101 us -> 0 us
  local copies, waits for them, and re-layouts: 97.1 us -> 1.06 us
  waiting for transfers between devices: 67.3 us -> 0 us
  matrix products: 60.1 us -> 0 us
  other arithmetic: 40.6 us -> 0 us
  starting transfers between devices: 17.7 us -> 0 us
    pallas_call x0 -> x1, Pallas kernels: none -> 121 us  [on_device(): pl.pallas_call(functools.partial(kernel, n_head), out_shape=pltpu.VMEM(sh...]
    all_to_all x2 -> x0, blocking collectives: 88.9 us -> none  [the longest x1 73.2 us: on_device(): lax.all_to_all(out_k, 'seq', split_axis=1, concat_axis=1, tiled=True)]
    all_to_all x4 -> x0, waiting for transfers between devices: 67.3 us -> none  [the longest x1 39 us: on_device(): lax.all_to_all(out_v, 'seq', split_axis=1, concat_axis=1, tiled=True)]
    dot_general x4 -> x0, matrix products: 60.1 us -> none  [the longest x2 31.4 us: tile_attention(): jnp.einsum('hqakb,hqkbd->hqad', weights, value_block, preferred_element_t...]
    gather x8 -> x0, local copies, waits for them, and re-layouts: 47.6 us -> none  [the longest x2 19.5 us: attend(): v_block = jnp.take(bank_v, index_block, axis=1)]
    reduce_sum x4 -> x0, other arithmetic: 22.1 us -> none  [the longest x2 21.5 us: tile_attention(): total = jnp.sum(weights.astype(jnp.float32), axis=(3, 4))]
    all_to_all x4 -> x0, starting transfers between devices: 17.7 us -> none  [the longest x1 5 us: on_device(): lax.all_to_all(out_v, 'seq', split_axis=1, concat_axis=1, tiled=True)]
    convert_element_type x5 -> x0, local copies, waits for them, and re-layouts: 14.2 us -> none  [the longest x2 7.81 us: on_device(): q_float = q_raw.astype(jnp.float32)]
  transfers between devices with their start and end apart: 4 -> 0, of which waited for: 3 -> 0; matrix products, arithmetic and copies ran while one was open for 9% -> 0% of each run, Pallas kernels for 0% -> 0%
where the time goes in v4:
time: 122 us
  Pallas kernels  121 us (99%)
    pallas_call x1, Pallas kernels, on_device(): pl.pallas_call(functools.partial(kernel, n_head), out_shape=pltpu.VMEM(sh...  121 us

profile of v4, /device:TPU:1, one launch (start us, length us, event | category | flops | bytes accessed | tf_op | source)
XLA Modules:
  0.0 121.9 jit_solution(4686947637411746648)
XLA Ops:
  0.0 120.8 %shard_map.82 = bf16[2,128,2560]{2,1,0:T(8,128)(2,1)S(1)} custom-call(s32[18,256]{1,0:T(8,128)} %bitcast.9, s32[256]{0:T(256)} %count_row.1, s32[256]{0:T(256)} %valid.1, bf16[2,128,2560]{2,1,0:T(8,128)(2,1)} %bitcast.6, bf16[2,128,2560]{2,1,0:T(8,128)(2,1)} %bitcast.7, bf16[2,128,2560]{2,1,0:T(8,128)(2,1)} %bitcast.8, f32[2560]{0:T(1024)} %gain_q.1, ...), custom_call_target="tpu_custom_call" | custom-call | tf_op jit(solution)/shard_map/pallas_call | solution.py:432
  120.8 1.1 copy.10

commit v5 on v4

--- a/solution.py
+++ b/solution.py
@@ -20,7 +20,7 @@
 COLUMNS = SIDE * SIDE
 HOPS = ((2, 0), (2, 1), (1, 0), (3, 0), (1, 1), (3, 1), (0, 1))
 CHUNKS = (0, 1, 3, 2)
-GROUPS = 4
+GROUPS = 8
 K, V, Q = 0, 1, 2
 
 
@@ -30,13 +30,13 @@
         + [("own_ring", V), ("own_ring", K), ("direct", K, 0), ("spread_v", 0)]
         + [("direct", K, q) for q in CHUNKS[1:]]
         + [("scale", Q), ("spread_q", 0), ("send", Q)]
-        + [("pass_on", K, 0), ("ring_rest", 0), ("direct", V, 0), ("pass_on", K, 1), ("pass_on", K, 3)]
-        + [("direct", V, 1), ("pass_on", K, 2), ("finish", K, 0), ("direct", V, 3), ("finish", K, 1)]
-        + [("relay", 0), ("direct", V, 2), ("finish", K, 3), ("finish", K, 2), ("pick", 0)]
-        + [("complete", K), ("weigh", 0), ("pass_on", V, 0), ("weigh", 1), ("pass_on", V, 1)]
-        + [("finish", V, 0), ("attend", 0), ("pass_on", V, 3), ("weigh", 2), ("pass_on", V, 2)]
-        + [("finish", V, 1), ("weigh", 3), ("finish", V, 3), ("finish", V, 2)]
-        + [("complete", V), ("mix", 0)]
+        + [("pass_on", K, 0), ("ring_rest", 0), ("pass_on", K, 1), ("pass_on", K, 3)]
+        + [("direct", V, 0), ("pass_on", K, 2), ("direct", V, 1), ("finish", K, 0), ("finish", K, 1)]
+        + [("direct", V, 3), ("relay", 0), ("finish", K, 3), ("direct", V, 2), ("finish", K, 2)]
+        + [("pick", 0), ("pass_on", V, 0), ("complete", K), ("weigh", 0), ("pass_on", V, 1)]
+        + [("weigh", 1), ("weigh", 2), ("weigh", 3), ("pass_on", V, 3), ("weigh", 4), ("weigh", 5)]
+        + [("pass_on", V, 2), ("finish", V, 0), ("finish", V, 1), ("weigh", 6), ("weigh", 7)]
+        + [("finish", V, 3), ("attend", 0), ("finish", V, 2), ("complete", V), ("mix", 0)]
     )
 
 
@@ -48,17 +48,27 @@
     return lax.rsqrt(jnp.sum(total, axis=-1, keepdims=True) / width + EPS)
 
 
-def find_wanted(s, place, span_tiles, listed_rows, count_row, found):
+def find_tables(s, place, span_tiles, own_tiles, last_valid, listed_rows, count_row, found, tables):
     slots, tiles = listed_rows.shape
     used = lax.broadcasted_iota(jnp.int32, (slots, tiles), 0) < count_row[...][None]
     listed = jnp.where(used, listed_rows[...], -1)
-    owner = listed >> (span_tiles.bit_length() - 1)
+    span_bits = span_tiles.bit_length() - 1
+    owner = listed >> span_bits
     tile = listed & (span_tiles - 1)
     for kind in (K, V):
         for a in range(SIDE):
             source = s + (a - place[kind]) * STRIDE[kind]
             best = jnp.max(jnp.where(owner == source, tile, 0), axis=0, keepdims=True)
             found[pl.ds(kind * SIDE + a, 1), :] = best
+    every = listed_rows[...]
+    spread = every & (tiles - 1)
+    z, y, c = spread >> (span_bits + 3), (spread >> (span_bits + 1)) & 3, (spread >> span_bits) & 1
+    own_bits = own_tiles.bit_length() - 1
+    column = (c * (span_tiles // own_tiles) + ((spread & (span_tiles - 1)) >> own_bits)) * COLUMNS + z * SIDE + y
+    tables[0] = column * own_tiles + (spread & (own_tiles - 1))
+    tables[1] = (y * CORES + c) * SIDE + z
+    tables[2] = (z * CORES + c) * SIDE + y
+    tables[3] = jnp.where(used, jnp.where(every == tiles - 1, last_valid, TILE), 0)
     best = found[...]
     for step in (1, 2, 4):
         best = jnp.maximum(best, pltpu.roll(best, tiles - step, 1))
@@ -67,9 +77,9 @@
 
 def kernel(
     n_head,
-    listed, counts, valid, q_hbm, k_hbm, v_hbm, gain_q, gain_k, listed_rows, count_row,
+    valid, q_hbm, k_hbm, v_hbm, gain_q, gain_k, listed_rows, count_row,
     o_ref,
-    q_in, k_in, q_norm, k_norm, found, wanted,
+    q_in, k_in, q_norm, k_norm, found, wanted, tables, look,
     col_k, col_v, col_q, col_out, weights, inverse,
     ring_k, ring_v, bank_k, bank_v, blk_q, picked, blk_out,
     in_sem, own_sem, m_send, m_recv, x_send, x_recv, c_send, c_recv,
@@ -84,8 +94,12 @@
     span_tiles = own_tiles * n_head
     half = span_tiles // 2
     width = q_hbm.shape[2]
-    slots = listed.shape[0]
+    slots, tiles = listed_rows.shape
     mine = pl.ds(x * own_tiles, own_tiles)
+
+    def slab(slot, first, count, lane=core):
+        return pl.ds(((lane * n_head + slot) * COLUMNS + first) * own_tiles, count * own_tiles)
+
     raw = (k_in, None, q_in)
     norm = (k_norm, None, q_norm)
     gain = (gain_k, None, gain_q)
@@ -126,7 +140,7 @@
         v_hbm.at[:, :, columns(rest_head)], ring_v.at[place[1], mine], own_sem.at[0]
     )
     own_col = pltpu.make_async_copy(
-        v_hbm.at[:, :, columns(here)], col_v.at[core, x, here], own_sem.at[1]
+        v_hbm.at[:, :, columns(here)], col_v.at[slab(x, here, 1)], own_sem.at[1]
     )
     own_rest.start()
     own_col.start()
@@ -137,9 +151,13 @@
     friends += [device(0, dy, 1) for dy in range(SIDE)] + [device(dz, 0, 1) for dz in range(1, SIDE)]
     for friend in friends:
         pl.semaphore_signal(barrier, inc=1, device_id=friend, device_id_type=MESH)
-    find_wanted(s, place, span_tiles, listed_rows, count_row, found)
+    find_tables(
+        s, place, span_tiles, own_tiles, valid[tiles - 1], listed_rows, count_row, found, tables
+    )
     to_smem = pltpu.make_async_copy(found, wanted, in_sem.at[2])
     to_smem.start()
+    tables_out = pltpu.make_async_copy(tables, look, in_sem.at[3])
+    tables_out.start()
     pl.semaphore_wait(barrier, len(friends))
 
     def scale(kind):
@@ -164,14 +182,14 @@
             for dy in CHUNKS:
                 if dz + dy:
                     z, y = lax.rem(place[0] + dz, SIDE), lax.rem(place[1] + dy, SIDE)
-                    landing = col_q.at[here] if kind == Q else col[kind].at[core, x, here]
+                    landing = col_q.at[here] if kind == Q else col[kind].at[slab(x, here, 1)]
                     remote(
                         source(kind, z * SIDE + y), landing, m_send.at[kind],
                         m_recv.at[kind, (SIDE - dz) % SIDE], device(dz, dy, 0),
                     )
 
     def spread_k(_):
-        col_k[core, x, here] = normalised(K, here)
+        col_k[slab(x, here, 1)] = normalised(K, here)
         to_columns(K)
 
     def spread_v(_):
@@ -181,43 +199,43 @@
         col_q[here] = normalised(Q, here)
         to_columns(Q)
 
-    def chunk_rows(q, first=0, count=SIDE):
-        return pl.ds(lax.rem(place[0] + q, SIDE) * SIDE + first, count)
+    def chunk(slot, q, first=0, count=SIDE):
+        return slab(slot, lax.rem(place[0] + q, SIDE) * SIDE + first, count)
 
     def chunk_wait(kind, q):
-        landed = col_k.at[0, 0, pl.ds(0, SIDE - 1 if q == 0 else SIDE)]
+        landed = col_k.at[pl.ds(0, (SIDE - 1 if q == 0 else SIDE) * own_tiles)]
         await_bytes(landed, m_recv.at[kind, q])
 
-    def across(kind, slot, rows):
-        ref = col[kind].at[core, slot, rows]
+    def across(kind, slot, q):
+        ref = col[kind].at[chunk(slot, q)]
         remote(ref, ref, c_send.at[kind], c_recv.at[kind], device(0, 0, 1))
 
     def direct(kind, q):
         if kind == V and q == 0:
             own_col.wait()
         chunk_wait(kind, q)
-        ref = col[kind].at[core, x, chunk_rows(q)]
+        ref = col[kind].at[chunk(x, q)]
         for n, along in enumerate((1, SIDE - 1)):
             remote(ref, ref, x_send.at[kind], x_recv.at[kind, n, q], beside(along))
-        across(kind, x, chunk_rows(q))
+        across(kind, x, q)
 
     def pass_on(kind, q):
         for n, along in enumerate((1, SIDE - 1)):
             slot = lax.rem(x + SIDE - along, SIDE)
-            await_bytes(col[kind].at[core, slot, chunk_rows(q)], x_recv.at[kind, n, q])
-            ref = col[kind].at[core, slot, chunk_rows(q, n * (SIDE // 2), SIDE // 2)]
+            await_bytes(col[kind].at[chunk(slot, q)], x_recv.at[kind, n, q])
+            ref = col[kind].at[chunk(slot, q, n * (SIDE // 2), SIDE // 2)]
             remote(ref, ref, x_send.at[kind], x_recv.at[kind, 2 + n, q], beside(along))
-            across(kind, slot, chunk_rows(q))
+            across(kind, slot, q)
 
     def finish(kind, q):
         slot = lax.rem(x + SIDE // 2, SIDE)
         for n in (0, 1):
-            ref = col[kind].at[core, slot, chunk_rows(q, n * (SIDE // 2), SIDE // 2)]
+            ref = col[kind].at[chunk(slot, q, n * (SIDE // 2), SIDE // 2)]
             await_bytes(ref, x_recv.at[kind, 2 + n, q])
-        across(kind, slot, chunk_rows(q))
+        across(kind, slot, q)
 
     def complete(kind):
-        await_bytes(col[kind].at[1 - core], c_recv.at[kind])
+        await_bytes(col[kind].at[slab(0, 0, n_head * COLUMNS, 1 - core)], c_recv.at[kind])
         if kind == K:
             for q in CHUNKS:
                 chunk_wait(Q, q)
@@ -225,12 +243,9 @@
     lane = lax.broadcasted_iota(jnp.int32, (1, TILE), 1)
 
     def key_bias(row):
-        count = counts[row]
-        bias = []
-        for e in range(slots):
-            limit = jnp.where(e < count, valid[listed[e, row]], 0)
-            bias.append(jnp.where(lane < limit, 0.0, MASKED))
-        return jnp.concatenate(bias, axis=1)
+        return jnp.concatenate(
+            [jnp.where(lane < look[3, e, row], 0.0, MASKED) for e in range(slots)], axis=1
+        )
 
     def softmax(query, keys, bias):
         scores = lax.dot_general(
@@ -240,10 +255,6 @@
         rows = jnp.exp2(scores - jnp.max(scores, axis=1, keepdims=True))
         return rows.astype(jnp.bfloat16), 1.0 / jnp.sum(rows, axis=1, keepdims=True)
 
-    def col_tile(ref, g):
-        block = g // span_tiles
-        return ref[block % CORES, g % span_tiles // own_tiles, block // CORES, g % own_tiles]
-
     def col_row(block, part):
         return (block * CORES + core) * span_tiles + x * own_tiles + part
 
@@ -254,7 +265,7 @@
         def _(block):
             for part in range(own_tiles):
                 row = col_row(block, part)
-                keys = [col_tile(col_k, listed[e, row]) for e in range(slots)]
+                keys = [col_k[look[0, e, row]] for e in range(slots)]
                 rows, inv = softmax(col_q[block, part], keys, key_bias(row))
                 weights[block, part] = rows
                 inverse[block, part] = inv
@@ -262,13 +273,13 @@
     def mix(_):
         @pl.loop(0, COLUMNS)
         def _(step):
-            off = COLUMNS - 1 - step
+            off = 5 * (step + 1) % COLUMNS
             dz, dy = off // SIDE, off % SIDE
             z, y = lax.rem(place[0] + dz, SIDE), lax.rem(place[1] + dy, SIDE)
             block = z * SIDE + y
             for part in range(own_tiles):
                 row = col_row(block, part)
-                vals = [col_tile(col_v, listed[e, row]) for e in range(slots)]
+                vals = [col_v[look[0, e, row]] for e in range(slots)]
                 mixed = jnp.dot(
                     weights[block, part], jnp.concatenate(vals, axis=0),
                     preferred_element_type=jnp.float32,
@@ -333,6 +344,7 @@
 
     def pick(_):
         to_smem.wait()
+        tables_out.wait()
         for kind in (K, V):
             for n in (0, 1):
                 await_bytes(ring[kind].at[0, pl.ds(0, half)], r_recv.at[kind, 2 + n])
@@ -342,12 +354,12 @@
                 for a in range(SIDE):
                     picked[kind, n, a] = ring[kind][a, wanted[kind * SIDE + a, dest[0] * span_tiles]]
                 remote(
-                    picked.at[kind, n], bank[kind].at[place[1 - kind] * CORES + core],
+                    picked.at[kind, n], bank[kind].at[pl.ds((place[1 - kind] * CORES + core) * SIDE, SIDE)],
                     b_send.at[kind], b_recv.at[kind], dest,
                 )
         for kind in (K, V):
             for a in range(SIDE):
-                bank[kind][place[1 - kind] * CORES + core, a] = ring[kind][
+                bank[kind][(place[1 - kind] * CORES + core) * SIDE + a] = ring[kind][
                     a, wanted[kind * SIDE + a, s * span_tiles]
                 ]
 
@@ -355,7 +367,7 @@
         for o in range(1, n_head):
             arrived(Q, o)
         for kind in (K, V):
-            await_bytes(bank[kind].at[pl.ds(0, len(HOPS))], b_recv.at[kind])
+            await_bytes(bank[kind].at[pl.ds(0, len(HOPS) * SIDE)], b_recv.at[kind])
 
         @pl.loop(0, span_tiles)
         def _(step):
@@ -368,10 +380,8 @@
             keys = [ring_k[place[K], i], ring_k[place[K], mate]]
             vals = [ring_v[place[V], i], ring_v[place[V], mate]]
             for e in range(2, slots):
-                owner = listed[e, row] // span_tiles
-                z, y, c = owner // STRIDE[0], owner // STRIDE[1] % SIDE, owner % CORES
-                keys.append(bank_k[y * CORES + c, z])
-                vals.append(bank_v[z * CORES + c, y])
+                keys.append(bank_k[look[1, e, row]])
+                vals.append(bank_v[look[2, e, row]])
             rows, inv = softmax(blk_q[i], keys, key_bias(row))
             mixed = jnp.dot(rows, jnp.concatenate(vals, axis=0), preferred_element_type=jnp.float32)
             blk_out[i] = (mixed * inv).astype(jnp.bfloat16)
@@ -399,8 +409,8 @@
         await_bytes(away, m_send.at[kind])
         await_bytes(aside, a_send.at[kind])
     for kind in (K, V):
-        await_bytes(col_k.at[0, pl.ds(0, 3)], x_send.at[kind])
-        await_bytes(col_k.at[0], c_send.at[kind])
+        await_bytes(col_k.at[slab(0, 0, 3 * COLUMNS, 0)], x_send.at[kind])
+        await_bytes(col_k.at[slab(0, 0, n_head * COLUMNS, 0)], c_send.at[kind])
         await_bytes(ring_k.at[pl.ds(0, 3)], r_send.at[kind])
         await_bytes(picked.at[kind], b_send.at[kind])
     for n, (moved, kept, head) in enumerate(
@@ -432,7 +442,7 @@
     out = pl.pallas_call(
         functools.partial(kernel, n_head),
         out_shape=pltpu.VMEM(shape, jnp.bfloat16),
-        in_specs=[smem] * 3 + [hbm] * 3 + [vmem] * 4,
+        in_specs=[smem] + [hbm] * 3 + [vmem] * 4,
         out_specs=hbm,
         scratch_shapes=[
             pltpu.VMEM(shape, jnp.bfloat16),
@@ -441,20 +451,22 @@
             buffer(heads, own_tiles),
             pltpu.VMEM((2 * SIDE, tiles), jnp.int32),
             pltpu.SMEM((2 * SIDE, tiles), jnp.int32),
-            buffer(CORES, n_head, COLUMNS, own_tiles),
-            buffer(CORES, n_head, COLUMNS, own_tiles),
+            pltpu.VMEM((4, slots, tiles), jnp.int32),
+            pltpu.SMEM((4, slots, tiles), jnp.int32),
+            buffer(tiles),
+            buffer(tiles),
             buffer(COLUMNS, own_tiles),
             buffer(COLUMNS, own_tiles),
             buffer(COLUMNS, own_tiles, tail=(TILE, slots * TILE)),
             buffer(COLUMNS, own_tiles, tail=(TILE, 1), kind=jnp.float32),
             buffer(SIDE, span_tiles),
             buffer(SIDE, span_tiles),
-            buffer(SIDE * CORES, SIDE),
-            buffer(SIDE * CORES, SIDE),
+            buffer(SIDE * CORES * SIDE),
+            buffer(SIDE * CORES * SIDE),
             buffer(span_tiles),
             buffer(2, len(HOPS), SIDE),
             buffer(span_tiles),
-            dma((3,)),
+            dma((4,)),
             dma((2,)),
             dma((3,)),
             dma((3, SIDE)),
@@ -476,7 +488,7 @@
             collective_id=0, has_side_effects=True, vmem_limit_bytes=58 << 20
         ),
     )(
-        listed, tile_counts, tile_valid,
+        tile_valid,
         queries.reshape(shape), keys.reshape(shape), values.reshape(shape),
         gain_q, gain_k, listed, tile_counts,
     )

time: 122 us -> 114 us (0.934)
  Pallas kernels: 121 us -> 113 us
    pallas_call x1, Pallas kernels: 121 us -> 113 us  [on_device(): pl.pallas_call(functools.partial(kernel, n_head), out_shape=pltpu.VMEM(sh...]
where the time goes in v5:
time: 114 us
  Pallas kernels  113 us (99%)
    pallas_call x1, Pallas kernels, on_device(): pl.pallas_call(functools.partial(kernel, n_head), out_shape=pltpu.VMEM(sh...  113 us

profile of v5, /device:TPU:1, one launch (start us, length us, event | category | flops | bytes accessed | tf_op | source)
XLA Modules:
  0.0 113.9 jit_solution(11909739579956778912)
XLA Ops:
  0.0 112.8 %shard_map.82 = bf16[2,128,2560]{2,1,0:T(8,128)(2,1)S(1)} custom-call(s32[256]{0:T(256)} %valid.1, bf16[2,128,2560]{2,1,0:T(8,128)(2,1)} %bitcast.6, bf16[2,128,2560]{2,1,0:T(8,128)(2,1)} %bitcast.7, bf16[2,128,2560]{2,1,0:T(8,128)(2,1)} %bitcast.8, f32[2560]{0:T(1024)} %gain_q.1, f32[2560]{0:T(1024)} %gain_k.1, s32[18,256]{1,0:T(8,128)} %bitcast.9, ...), custom_call_target="tpu_custom_call" | custom-call | tf_op jit(solution)/shard_map/pallas_call | solution.py:442
  112.8 1.1 copy.10

commit v6 on v5

--- a/solution.py
+++ b/solution.py
@@ -26,17 +26,18 @@
 
 def schedule():
     return (
-        [("send", V), ("scale", K), ("spread_k", 0), ("send", K)]
-        + [("own_ring", V), ("own_ring", K), ("direct", K, 0), ("spread_v", 0)]
-        + [("direct", K, q) for q in CHUNKS[1:]]
-        + [("scale", Q), ("spread_q", 0), ("send", Q)]
+        [("send", V), ("early", V), ("spread_v", 0), ("own_ring", V), ("scale", K), ("own", K), ("early", K)]
+        + [("send", K), ("spread_k", 0), ("own_ring", K), ("direct", V, 0), ("look_up", 0)]
+        + [("direct", K, q) for q in CHUNKS]
+        + [("spread_v", 1), ("spread_v", 3), ("spread_v", 2)]
         + [("pass_on", K, 0), ("ring_rest", 0), ("pass_on", K, 1), ("pass_on", K, 3)]
-        + [("direct", V, 0), ("pass_on", K, 2), ("direct", V, 1), ("finish", K, 0), ("finish", K, 1)]
-        + [("direct", V, 3), ("relay", 0), ("finish", K, 3), ("direct", V, 2), ("finish", K, 2)]
+        + [("scale", Q), ("own", Q), ("spread_q", 0), ("send", Q)]
+        + [("direct", V, 1), ("pass_on", K, 2), ("direct", V, 3), ("finish", K, 0), ("finish", K, 1)]
+        + [("relay", 0), ("finish", K, 3), ("direct", V, 2), ("finish", K, 2)]
         + [("pick", 0), ("pass_on", V, 0), ("complete", K), ("weigh", 0), ("pass_on", V, 1)]
-        + [("weigh", 1), ("weigh", 2), ("weigh", 3), ("pass_on", V, 3), ("weigh", 4), ("weigh", 5)]
-        + [("pass_on", V, 2), ("finish", V, 0), ("finish", V, 1), ("weigh", 6), ("weigh", 7)]
-        + [("finish", V, 3), ("attend", 0), ("finish", V, 2), ("complete", V), ("mix", 0)]
+        + [("weigh", 1), ("weigh", 2), ("pass_on", V, 3), ("weigh", 3), ("weigh", 4), ("pass_on", V, 2)]
+        + [("attend", 0), ("answer", 0), ("finish", V, 0), ("finish", V, 1), ("weigh", 5), ("weigh", 6), ("weigh", 7)]
+        + [("finish", V, 3), ("finish", V, 2), ("complete", V), ("mix", 0)]
     )
 
 
@@ -77,8 +78,9 @@
 
 def kernel(
     n_head,
-    valid, q_hbm, k_hbm, v_hbm, gain_q, gain_k, listed_rows, count_row,
+    valid_hbm, q_hbm, k_hbm, v_hbm, gain_q_hbm, gain_k_hbm, listed_hbm, count_hbm,
     o_ref,
+    valid, gain_q, gain_k, listed_rows, count_row, small_sem,
     q_in, k_in, q_norm, k_norm, found, wanted, tables, look,
     col_k, col_v, col_q, col_out, weights, inverse,
     ring_k, ring_v, bank_k, bank_v, blk_q, picked, blk_out,
@@ -132,8 +134,23 @@
         pltpu.make_async_copy(ref, ref, sem).wait()
 
     load_k = pltpu.make_async_copy(k_hbm, k_in, in_sem.at[0])
+    load_k.start()
+    barrier = pltpu.get_barrier_semaphore()
+    friends = [beside(o) for o in range(1, n_head)]
+    friends += [device(dz, dy, 0) for dz in range(SIDE) for dy in range(SIDE) if dz + dy]
+    friends += [device(0, dy, 1) for dy in range(SIDE)] + [device(dz, 0, 1) for dz in range(1, SIDE)]
+    for friend in friends:
+        pl.semaphore_signal(barrier, inc=1, device_id=friend, device_id_type=MESH)
+    small = [
+        pltpu.make_async_copy(src, dst, small_sem.at[n])
+        for n, (src, dst) in enumerate((
+            (gain_k_hbm, gain_k), (listed_hbm, listed_rows), (count_hbm, count_row),
+            (valid_hbm, valid), (gain_q_hbm, gain_q),
+        ))
+    ]
+    for copy in small:
+        copy.start()
     load_q = pltpu.make_async_copy(q_hbm, q_in, in_sem.at[1])
-    load_k.start()
     load_q.start()
     rest_head = COLUMNS + x
     own_rest = pltpu.make_async_copy(
@@ -145,23 +162,23 @@
     own_rest.start()
     own_col.start()
 
-    barrier = pltpu.get_barrier_semaphore()
-    friends = [beside(o) for o in range(1, n_head)]
-    friends += [device(dz, dy, 0) for dz in range(SIDE) for dy in range(SIDE) if dz + dy]
-    friends += [device(0, dy, 1) for dy in range(SIDE)] + [device(dz, 0, 1) for dz in range(1, SIDE)]
-    for friend in friends:
-        pl.semaphore_signal(barrier, inc=1, device_id=friend, device_id_type=MESH)
-    find_tables(
-        s, place, span_tiles, own_tiles, valid[tiles - 1], listed_rows, count_row, found, tables
-    )
+    pl.semaphore_wait(barrier, len(friends))
+
     to_smem = pltpu.make_async_copy(found, wanted, in_sem.at[2])
-    to_smem.start()
     tables_out = pltpu.make_async_copy(tables, look, in_sem.at[3])
-    tables_out.start()
-    pl.semaphore_wait(barrier, len(friends))
+
+    def look_up(_):
+        for copy in small[1:4]:
+            copy.wait()
+        find_tables(
+            s, place, span_tiles, own_tiles, valid[tiles - 1], listed_rows, count_row, found, tables
+        )
+        to_smem.start()
+        tables_out.start()
 
     def scale(kind):
         (load_k if kind == K else load_q).wait()
+        small[0 if kind == K else 4].wait()
         scales[kind] = row_scale(raw[kind], width)
         if kind == Q:
             scales[kind] = scales[kind] * (HD**-0.5 * LOG2E)
@@ -177,27 +194,33 @@
         norm[kind][head] = normalised(kind, head)
         return norm[kind].at[head]
 
-    def to_columns(kind):
-        for dz in CHUNKS:
-            for dy in CHUNKS:
-                if dz + dy:
-                    z, y = lax.rem(place[0] + dz, SIDE), lax.rem(place[1] + dy, SIDE)
-                    landing = col_q.at[here] if kind == Q else col[kind].at[slab(x, here, 1)]
-                    remote(
-                        source(kind, z * SIDE + y), landing, m_send.at[kind],
-                        m_recv.at[kind, (SIDE - dz) % SIDE], device(dz, dy, 0),
-                    )
+    def to_columns(kind, q):
+        dz = (SIDE - q) % SIDE
+        for dy in CHUNKS:
+            if dz + dy:
+                z, y = lax.rem(place[0] + dz, SIDE), lax.rem(place[1] + dy, SIDE)
+                landing = col_q.at[here] if kind == Q else col[kind].at[slab(x, here, 1)]
+                remote(
+                    source(kind, z * SIDE + y), landing, m_send.at[kind],
+                    m_recv.at[kind, q], device(dz, dy, 0),
+                )
+
+    def own(kind):
+        if kind == K:
+            col_k[slab(x, here, 1)] = normalised(K, here)
+        else:
+            col_q[here] = normalised(Q, here)
 
     def spread_k(_):
-        col_k[slab(x, here, 1)] = normalised(K, here)
-        to_columns(K)
-
-    def spread_v(_):
-        to_columns(V)
+        for q in CHUNKS:
+            to_columns(K, q)
+
+    def spread_v(q):
+        to_columns(V, q)
 
     def spread_q(_):
-        col_q[here] = normalised(Q, here)
-        to_columns(Q)
+        for q in CHUNKS:
+            to_columns(Q, q)
 
     def chunk(slot, q, first=0, count=SIDE):
         return slab(slot, lax.rem(place[0] + q, SIDE) * SIDE + first, count)
@@ -210,13 +233,23 @@
         ref = col[kind].at[chunk(slot, q)]
         remote(ref, ref, c_send.at[kind], c_recv.at[kind], device(0, 0, 1))
 
-    def direct(kind, q):
-        if kind == V and q == 0:
-            own_col.wait()
-        chunk_wait(kind, q)
-        ref = col[kind].at[chunk(x, q)]
+    def around(kind, q, rows):
+        ref = col[kind].at[rows]
         for n, along in enumerate((1, SIDE - 1)):
             remote(ref, ref, x_send.at[kind], x_recv.at[kind, n, q], beside(along))
+
+    def early(kind):
+        if kind == V:
+            own_col.wait()
+        around(kind, 0, slab(x, here, 1))
+
+    def direct(kind, q):
+        chunk_wait(kind, q)
+        if q == 0:
+            for dy in (1, 3, 2):
+                around(kind, q, slab(x, place[0] * SIDE + lax.rem(place[1] + dy, SIDE), 1))
+        else:
+            around(kind, q, chunk(x, q))
         across(kind, x, q)
 
     def pass_on(kind, q):
@@ -371,10 +404,7 @@
 
         @pl.loop(0, span_tiles)
         def _(step):
-            o = n_head - 1 - step // own_tiles
-            part = step % own_tiles
-            dest = lax.rem(x + o, n_head)
-            i = dest * own_tiles + part
+            i = step
             row = s * span_tiles + i
             mate = i + 1 - 2 * (i % 2)
             keys = [ring_k[place[K], i], ring_k[place[K], mate]]
@@ -386,17 +416,17 @@
             mixed = jnp.dot(rows, jnp.concatenate(vals, axis=0), preferred_element_type=jnp.float32)
             blk_out[i] = (mixed * inv).astype(jnp.bfloat16)
 
-            @pl.when((part == own_tiles - 1) & (o > 0))
-            def _():
-                remote(
-                    blk_out.at[pl.ds(dest * own_tiles, own_tiles)], o_ref.at[:, :, columns(rest_head)],
-                    o_send.at[1], o_recv.at[1], (s, dest),
-                )
-
+    def answer(_):
+        for o in (2, 1, 3):
+            dest = lax.rem(x + o, n_head)
+            remote(
+                blk_out.at[pl.ds(dest * own_tiles, own_tiles)], o_ref.at[:, :, columns(rest_head)],
+                o_send.at[1], o_recv.at[1], beside(o),
+            )
         pltpu.make_async_copy(blk_out.at[mine], o_ref.at[:, :, columns(rest_head)], o_own.at[1]).start()
 
     stages = dict(
-        send=send, scale=scale, spread_k=spread_k, spread_v=spread_v, spread_q=spread_q,
+        send=send, scale=scale, look_up=look_up, answer=answer, own=own, early=early, spread_k=spread_k, spread_v=spread_v, spread_q=spread_q,
         own_ring=own_ring, direct=direct, pass_on=pass_on, finish=finish, complete=complete,
         ring_rest=ring_rest, relay=relay, pick=pick, weigh=weigh, attend=attend, mix=mix,
     )
@@ -430,8 +460,6 @@
     tiles, slots = key_tiles.shape
     listed = key_tiles.T
 
-    smem = pl.BlockSpec(memory_space=pltpu.SMEM)
-    vmem = pl.BlockSpec(memory_space=pltpu.VMEM)
     hbm = pl.BlockSpec(memory_space=pl.ANY)
     shape = (own_tiles, TILE, width)
     dma = pltpu.SemaphoreType.DMA
@@ -442,9 +470,15 @@
     out = pl.pallas_call(
         functools.partial(kernel, n_head),
         out_shape=pltpu.VMEM(shape, jnp.bfloat16),
-        in_specs=[smem] + [hbm] * 3 + [vmem] * 4,
+        in_specs=[hbm] * 8,
         out_specs=hbm,
         scratch_shapes=[
+            pltpu.SMEM((tiles,), jnp.int32),
+            pltpu.VMEM((width,), jnp.float32),
+            pltpu.VMEM((width,), jnp.float32),
+            pltpu.VMEM((slots, tiles), jnp.int32),
+            pltpu.VMEM((tiles,), jnp.int32),
+            pltpu.SemaphoreType.DMA((5,)),
             pltpu.VMEM(shape, jnp.bfloat16),
             pltpu.VMEM(shape, jnp.bfloat16),
             buffer(heads, own_tiles),

time: 114 us -> 110 us (0.965)
  Pallas kernels: 113 us -> 109 us
    pallas_call x1, Pallas kernels: 113 us -> 109 us  [on_device(): pl.pallas_call(functools.partial(kernel, n_head), out_shape=pltpu.VMEM(sh...]
where the time goes in v6:
time: 110 us
  Pallas kernels  109 us (99%)
    pallas_call x1, Pallas kernels, on_device(): pl.pallas_call(functools.partial(kernel, n_head), out_shape=pltpu.VMEM(sh...  109 us

profile of v6, /device:TPU:1, one launch (start us, length us, event | category | flops | bytes accessed | tf_op | source)
XLA Modules:
  0.0 110.0 jit_solution(10312431772102053973)
XLA Ops:
  0.0 109.0 %shard_map.82 = bf16[2,128,2560]{2,1,0:T(8,128)(2,1)S(1)} custom-call(s32[256]{0:T(256)} %valid_hbm.1, bf16[2,128,2560]{2,1,0:T(8,128)(2,1)} %bitcast.6, bf16[2,128,2560]{2,1,0:T(8,128)(2,1)} %bitcast.7, bf16[2,128,2560]{2,1,0:T(8,128)(2,1)} %bitcast.8, f32[2560]{0:T(1024)} %gain_q_hbm.1, f32[2560]{0:T(1024)} %gain_k_hbm.1, s32[18,256]{1,0:T(8,128)} %bitcast.9, ...), custom_call_target="tpu_custom_call" | custom-call | tf_op jit(solution)/shard_map/pallas_call | solution.py:470
  109.0 1.1 copy.10

commit v7 on v6

--- a/solution.py
+++ b/solution.py
@@ -21,23 +21,29 @@
 HOPS = ((2, 0), (2, 1), (1, 0), (3, 0), (1, 1), (3, 1), (0, 1))
 CHUNKS = (0, 1, 3, 2)
 GROUPS = 8
-K, V, Q = 0, 1, 2
+K, V, Q, W = 0, 1, 2, 3
+HALF = HD // 2
 
 
 def schedule():
     return (
-        [("send", V), ("early", V), ("spread_v", 0), ("own_ring", V), ("scale", K), ("own", K), ("early", K)]
-        + [("send", K), ("spread_k", 0), ("own_ring", K), ("direct", V, 0), ("look_up", 0)]
+        [("send", V), ("scale", K), ("own", K), ("early", K), ("send", K), ("spread_k", 0)]
+        + [("own_ring", V), ("own_ring", K), ("look_up", 0)]
         + [("direct", K, q) for q in CHUNKS]
-        + [("spread_v", 1), ("spread_v", 3), ("spread_v", 2)]
+        + [("halve", 0)] + [("spread_v", V, q) for q in CHUNKS]
         + [("pass_on", K, 0), ("ring_rest", 0), ("pass_on", K, 1), ("pass_on", K, 3)]
         + [("scale", Q), ("own", Q), ("spread_q", 0), ("send", Q)]
-        + [("direct", V, 1), ("pass_on", K, 2), ("direct", V, 3), ("finish", K, 0), ("finish", K, 1)]
-        + [("relay", 0), ("finish", K, 3), ("direct", V, 2), ("finish", K, 2)]
-        + [("pick", 0), ("pass_on", V, 0), ("complete", K), ("weigh", 0), ("pass_on", V, 1)]
-        + [("weigh", 1), ("weigh", 2), ("pass_on", V, 3), ("weigh", 3), ("weigh", 4), ("pass_on", V, 2)]
-        + [("attend", 0), ("answer", 0), ("finish", V, 0), ("finish", V, 1), ("weigh", 5), ("weigh", 6), ("weigh", 7)]
-        + [("finish", V, 3), ("finish", V, 2), ("complete", V), ("mix", 0)]
+        + [("direct", V, 0), ("pass_on", K, 2), ("direct", V, 1), ("finish", K, 0), ("finish", K, 1)]
+        + [("spread_v", W, q) for q in CHUNKS]
+        + [("direct", V, 3), ("relay", 0), ("finish", K, 3), ("direct", V, 2), ("finish", K, 2)]
+        + [("pick", 0), ("pass_on", V, 0), ("direct", W, 0), ("complete", K), ("weigh", 0)]
+        + [("pass_on", V, 1), ("direct", W, 1), ("weigh", 1), ("pass_on", V, 3), ("direct", W, 3), ("weigh", 2)]
+        + [("pass_on", V, 2), ("direct", W, 2), ("weigh", 3), ("finish", V, 0), ("finish", V, 1), ("weigh", 4)]
+        + [("attend", 0), ("pass_on", W, 0), ("finish", V, 3), ("weigh", 5), ("finish", V, 2), ("weigh", 6), ("weigh", 7)]
+        + [("pass_on", W, 1), ("pass_on", W, 3), ("pass_on", W, 2), ("answer", 0)]
+        + [("complete", V), ("mix", V, 0), ("finish", W, 0), ("mix", V, 1)]
+        + [("finish", W, 1), ("finish", W, 3), ("finish", W, 2)]
+        + [("complete", W), ("mix", W, 0), ("mix", W, 1), ("join", 0)]
     )
 
 
@@ -81,8 +87,8 @@
     valid_hbm, q_hbm, k_hbm, v_hbm, gain_q_hbm, gain_k_hbm, listed_hbm, count_hbm,
     o_ref,
     valid, gain_q, gain_k, listed_rows, count_row, small_sem,
-    q_in, k_in, q_norm, k_norm, found, wanted, tables, look,
-    col_k, col_v, col_q, col_out, weights, inverse,
+    q_in, k_in, v_in, q_norm, k_norm, v_half, found, wanted, tables, look,
+    col_k, col_v, col_w, col_q, col_out, landed, weights, inverse,
     ring_k, ring_v, bank_k, bank_v, blk_q, picked, blk_out,
     in_sem, own_sem, m_send, m_recv, x_send, x_recv, c_send, c_recv,
     a_send, a_recv, r_send, r_recv, b_send, b_recv, o_send, o_recv, o_own,
@@ -105,7 +111,7 @@
     raw = (k_in, None, q_in)
     norm = (k_norm, None, q_norm)
     gain = (gain_k, None, gain_q)
-    col = (col_k, col_v, col_q)
+    col = (col_k, col_v, col_q, col_w)
     ring = (ring_k, ring_v)
     bank = (bank_k, bank_v)
     scales = {}
@@ -156,11 +162,9 @@
     own_rest = pltpu.make_async_copy(
         v_hbm.at[:, :, columns(rest_head)], ring_v.at[place[1], mine], own_sem.at[0]
     )
-    own_col = pltpu.make_async_copy(
-        v_hbm.at[:, :, columns(here)], col_v.at[slab(x, here, 1)], own_sem.at[1]
-    )
+    load_v = pltpu.make_async_copy(v_hbm, v_in, own_sem.at[1])
     own_rest.start()
-    own_col.start()
+    load_v.start()
 
     pl.semaphore_wait(barrier, len(friends))
 
@@ -200,8 +204,10 @@
             if dz + dy:
                 z, y = lax.rem(place[0] + dz, SIDE), lax.rem(place[1] + dy, SIDE)
                 landing = col_q.at[here] if kind == Q else col[kind].at[slab(x, here, 1)]
+                head = z * SIDE + y
+                part = v_half.at[kind // W, head] if kind in (V, W) else source(kind, head)
                 remote(
-                    source(kind, z * SIDE + y), landing, m_send.at[kind],
+                    part, landing, m_send.at[kind],
                     m_recv.at[kind, q], device(dz, dy, 0),
                 )
 
@@ -215,8 +221,23 @@
         for q in CHUNKS:
             to_columns(K, q)
 
-    def spread_v(q):
-        to_columns(V, q)
+    def halve(_):
+        load_v.wait()
+        shape = (2 * HD, 2 * HD)
+        i, j = lax.broadcasted_iota(jnp.int32, shape, 0), lax.broadcasted_iota(jnp.int32, shape, 1)
+        target = i % HALF + HALF * (i // HD) + HD * (i // HALF % 2)
+        mover = jnp.where(j == target, 1.0, 0.0).astype(jnp.bfloat16)
+        for head in range(COLUMNS):
+            rows = v_in[:, :, head * HD : (head + 1) * HD]
+            rows = jnp.concatenate([rows[:, :HALF], rows[:, HALF:]], axis=2).reshape(own_tiles * HALF, 2 * HD)
+            moved = jnp.dot(rows, mover, preferred_element_type=jnp.float32).astype(jnp.bfloat16)
+            for n in (0, 1):
+                v_half[n, head] = moved[:, n * HD : (n + 1) * HD].reshape(own_tiles, HALF, HD)
+        for n, ref in enumerate((col_v, col_w)):
+            ref[slab(x, here, 1)] = v_half[n, here]
+
+    def spread_v(kind, q):
+        to_columns(kind, q)
 
     def spread_q(_):
         for q in CHUNKS:
@@ -226,8 +247,8 @@
         return slab(slot, lax.rem(place[0] + q, SIDE) * SIDE + first, count)
 
     def chunk_wait(kind, q):
-        landed = col_k.at[pl.ds(0, (SIDE - 1 if q == 0 else SIDE) * own_tiles)]
-        await_bytes(landed, m_recv.at[kind, q])
+        arrived_tiles = pl.ds(0, (SIDE - 1 if q == 0 else SIDE) * own_tiles)
+        await_bytes((col_k if kind == Q else col[kind]).at[arrived_tiles], m_recv.at[kind, q])
 
     def across(kind, slot, q):
         ref = col[kind].at[chunk(slot, q)]
@@ -239,13 +260,11 @@
             remote(ref, ref, x_send.at[kind], x_recv.at[kind, n, q], beside(along))
 
     def early(kind):
-        if kind == V:
-            own_col.wait()
         around(kind, 0, slab(x, here, 1))
 
     def direct(kind, q):
         chunk_wait(kind, q)
-        if q == 0:
+        if kind == K and q == 0:
             for dy in (1, 3, 2):
                 around(kind, q, slab(x, place[0] * SIDE + lax.rem(place[1] + dy, SIDE), 1))
         else:
@@ -280,6 +299,21 @@
             [jnp.where(lane < look[3, e, row], 0.0, MASKED) for e in range(slots)], axis=1
         )
 
+    def folded_bias(row):
+        parts = []
+        for e in range(0, slots, 2):
+            limit = jnp.where(lane < HALF, look[3, e, row], look[3, e + 1, row])
+            for first in (0, HALF):
+                parts.append(jnp.where(lane % HALF + first < limit, 0.0, MASKED))
+        return jnp.concatenate(parts, axis=1)
+
+    def folded_keys(row):
+        parts = []
+        for e in range(0, slots, 2):
+            pair = [col_k[look[0, e + n, row]] for n in (0, 1)]
+            parts += [tile[first : first + HALF] for first in (0, HALF) for tile in pair]
+        return parts
+
     def softmax(query, keys, bias):
         scores = lax.dot_general(
             query, jnp.concatenate(keys, axis=0), (((1,), (1,)), ((), ())),
@@ -298,35 +332,60 @@
         def _(block):
             for part in range(own_tiles):
                 row = col_row(block, part)
-                keys = [col_k[look[0, e, row]] for e in range(slots)]
-                rows, inv = softmax(col_q[block, part], keys, key_bias(row))
+                rows, inv = softmax(col_q[block, part], folded_keys(row), folded_bias(row))
                 weights[block, part] = rows
                 inverse[block, part] = inv
 
-    def mix(_):
-        @pl.loop(0, COLUMNS)
+    def mix(kind, turn):
+        wide = lax.broadcasted_iota(jnp.int32, (TILE, HD), 1)
+
+        def fold(block, part):
+            row = col_row(block, part)
+            vals = jnp.concatenate([col[kind][look[0, e, row]] for e in range(slots)], axis=0)
+            rows = weights[block, part]
+            low, high = [
+                jnp.dot(
+                    jnp.concatenate(
+                        [rows[:, m : m + TILE] for m in range(n * TILE, slots * TILE, 2 * TILE)], axis=1
+                    ),
+                    vals, preferred_element_type=jnp.float32,
+                )
+                for n in (0, 1)
+            ]
+            if part == 0:
+                both = low + pltpu.roll(high, HALF, 1)
+            else:
+                both = pltpu.roll(low, HALF, 1) + high
+            return both * inverse[block, part]
+
+        @pl.loop(turn * COLUMNS // 2, (turn + 1) * COLUMNS // 2)
         def _(step):
             off = 5 * (step + 1) % COLUMNS
             dz, dy = off // SIDE, off % SIDE
             z, y = lax.rem(place[0] + dz, SIDE), lax.rem(place[1] + dy, SIDE)
             block = z * SIDE + y
-            for part in range(own_tiles):
-                row = col_row(block, part)
-                vals = [col_v[look[0, e, row]] for e in range(slots)]
-                mixed = jnp.dot(
-                    weights[block, part], jnp.concatenate(vals, axis=0),
-                    preferred_element_type=jnp.float32,
-                )
-                col_out[block, part] = (mixed * inverse[block, part]).astype(jnp.bfloat16)
+            mixed = jnp.where(wide < HALF, fold(block, 0), fold(block, 1)).astype(jnp.bfloat16)
+            col_out[kind // W, block] = mixed
 
             @pl.when(off > 0)
             def _():
                 remote(
-                    col_out.at[block], o_ref.at[:, :, columns(here)], o_send.at[0], o_recv.at[0],
+                    col_out.at[kind // W, block], landed.at[kind // W, here],
+                    o_send.at[kind // W], o_recv.at[kind // W],
                     (z * STRIDE[0] + y * STRIDE[1] + core, x),
                 )
 
-        pltpu.make_async_copy(col_out.at[here], o_ref.at[:, :, columns(here)], o_own.at[0]).start()
+    def join(_):
+        away = landed.at[0, pl.ds(0, COLUMNS - 1)]
+        for n in (0, 1):
+            await_bytes(away, o_recv.at[n])
+            landed[n, here] = col_out[n, here]
+        wide = lax.broadcasted_iota(jnp.int32, (TILE, HD), 1)
+        for head in range(COLUMNS):
+            low, high = [landed[n, head].astype(jnp.float32) for n in (0, 1)]
+            cols = slice(head * HD, (head + 1) * HD)
+            o_ref[0, :, cols] = jnp.where(wide < HALF, low, pltpu.roll(high, HALF, 1)).astype(jnp.bfloat16)
+            o_ref[1, :, cols] = jnp.where(wide < HALF, pltpu.roll(low, HALF, 1), high).astype(jnp.bfloat16)
 
     def home(kind):
         return blk_q if kind == Q else ring[kind].at[place[kind]]
@@ -421,34 +480,35 @@
             dest = lax.rem(x + o, n_head)
             remote(
                 blk_out.at[pl.ds(dest * own_tiles, own_tiles)], o_ref.at[:, :, columns(rest_head)],
-                o_send.at[1], o_recv.at[1], beside(o),
+                o_send.at[2], o_recv.at[2], beside(o),
             )
-        pltpu.make_async_copy(blk_out.at[mine], o_ref.at[:, :, columns(rest_head)], o_own.at[1]).start()
+        pltpu.make_async_copy(blk_out.at[mine], o_ref.at[:, :, columns(rest_head)], o_own.at[0]).start()
 
     stages = dict(
-        send=send, scale=scale, look_up=look_up, answer=answer, own=own, early=early, spread_k=spread_k, spread_v=spread_v, spread_q=spread_q,
+        send=send, scale=scale, look_up=look_up, answer=answer, own=own, early=early, spread_k=spread_k, spread_v=spread_v, halve=halve, join=join, spread_q=spread_q,
         own_ring=own_ring, direct=direct, pass_on=pass_on, finish=finish, complete=complete,
         ring_rest=ring_rest, relay=relay, pick=pick, weigh=weigh, attend=attend, mix=mix,
     )
     for name, *args in schedule():
         stages[name](*args)
 
-    away = col_q.at[pl.ds(0, COLUMNS - 1)]
+    away = pl.ds(0, (COLUMNS - 1) * own_tiles)
     aside = blk_q.at[pl.ds(0, span_tiles - own_tiles)]
+    for kind in (K, V, Q, W):
+        await_bytes((col_k if kind == Q else col[kind]).at[away], m_send.at[kind])
     for kind in (K, V, Q):
-        await_bytes(away, m_send.at[kind])
         await_bytes(aside, a_send.at[kind])
+    for kind in (K, V, W):
+        await_bytes(col[kind].at[slab(0, 0, 3 * COLUMNS, 0)], x_send.at[kind])
+        await_bytes(col[kind].at[slab(0, 0, n_head * COLUMNS, 0)], c_send.at[kind])
     for kind in (K, V):
-        await_bytes(col_k.at[slab(0, 0, 3 * COLUMNS, 0)], x_send.at[kind])
-        await_bytes(col_k.at[slab(0, 0, n_head * COLUMNS, 0)], c_send.at[kind])
         await_bytes(ring_k.at[pl.ds(0, 3)], r_send.at[kind])
         await_bytes(picked.at[kind], b_send.at[kind])
-    for n, (moved, kept, head) in enumerate(
-        ((away, col_out.at[here], here), (aside, blk_out.at[mine], rest_head))
-    ):
-        await_bytes(moved, o_send.at[n])
-        await_bytes(moved, o_recv.at[n])
-        pltpu.make_async_copy(kept, o_ref.at[:, :, columns(head)], o_own.at[n]).wait()
+    for n in (0, 1):
+        await_bytes(landed.at[0, pl.ds(0, COLUMNS - 1)], o_send.at[n])
+    await_bytes(aside, o_send.at[2])
+    await_bytes(aside, o_recv.at[2])
+    pltpu.make_async_copy(blk_out.at[mine], o_ref.at[:, :, columns(rest_head)], o_own.at[0]).wait()
 
 
 def on_device(queries, keys, values, gain_q, gain_k, key_tiles, tile_counts, tile_valid):
@@ -471,7 +531,7 @@
         functools.partial(kernel, n_head),
         out_shape=pltpu.VMEM(shape, jnp.bfloat16),
         in_specs=[hbm] * 8,
-        out_specs=hbm,
+        out_specs=pl.BlockSpec(memory_space=pltpu.VMEM),
         scratch_shapes=[
             pltpu.SMEM((tiles,), jnp.int32),
             pltpu.VMEM((width,), jnp.float32),
@@ -481,16 +541,20 @@
             pltpu.SemaphoreType.DMA((5,)),
             pltpu.VMEM(shape, jnp.bfloat16),
             pltpu.VMEM(shape, jnp.bfloat16),
+            pltpu.VMEM(shape, jnp.bfloat16),
             buffer(heads, own_tiles),
             buffer(heads, own_tiles),
+            buffer(2, COLUMNS, own_tiles, tail=(HALF, HD)),
             pltpu.VMEM((2 * SIDE, tiles), jnp.int32),
             pltpu.SMEM((2 * SIDE, tiles), jnp.int32),
             pltpu.VMEM((4, slots, tiles), jnp.int32),
             pltpu.SMEM((4, slots, tiles), jnp.int32),
             buffer(tiles),
-            buffer(tiles),
+            buffer(tiles, tail=(HALF, HD)),
+            buffer(tiles, tail=(HALF, HD)),
             buffer(COLUMNS, own_tiles),
-            buffer(COLUMNS, own_tiles),
+            buffer(2, COLUMNS),
+            buffer(2, COLUMNS),
             buffer(COLUMNS, own_tiles, tail=(TILE, slots * TILE)),
             buffer(COLUMNS, own_tiles, tail=(TILE, 1), kind=jnp.float32),
             buffer(SIDE, span_tiles),
@@ -502,21 +566,21 @@
             buffer(span_tiles),
             dma((4,)),
             dma((2,)),
-            dma((3,)),
-            dma((3, SIDE)),
-            dma((2,)),
-            dma((2, 4, SIDE)),
-            dma((2,)),
-            dma((2,)),
+            dma((4,)),
+            dma((4, SIDE)),
+            dma((4,)),
+            dma((4, 4, SIDE)),
+            dma((4,)),
+            dma((4,)),
             dma((3,)),
             dma((3, n_head - 1)),
             dma((2,)),
             dma((2, 4)),
             dma((2,)),
             dma((2,)),
-            dma((2,)),
-            dma((2,)),
-            dma((2,)),
+            dma((3,)),
+            dma((3,)),
+            dma((1,)),
         ],
         compiler_params=pltpu.CompilerParams(
             collective_id=0, has_side_effects=True, vmem_limit_bytes=58 << 20

time: 110 us -> 107 us (0.973)
  Pallas kernels: 109 us -> 106 us
    pallas_call x1, Pallas kernels: 109 us -> 106 us  [on_device(): pl.pallas_call(functools.partial(kernel, n_head), out_shape=pltpu.VMEM(sh...]
where the time goes in v7:
time: 107 us
  Pallas kernels  106 us (99%)
    pallas_call x1, Pallas kernels, on_device(): pl.pallas_call(functools.partial(kernel, n_head), out_shape=pltpu.VMEM(sh...  106 us

profile of v7, /device:TPU:1, one launch (start us, length us, event | category | flops | bytes accessed | tf_op | source)
XLA Modules:
  0.0 107.3 jit_solution(14185825368523747654)
XLA Ops:
  0.0 106.2 %shard_map.82 = bf16[2,128,2560]{2,1,0:T(8,128)(2,1)S(1)} custom-call(s32[256]{0:T(256)} %valid_hbm.1, bf16[2,128,2560]{2,1,0:T(8,128)(2,1)} %bitcast.6, bf16[2,128,2560]{2,1,0:T(8,128)(2,1)} %bitcast.7, bf16[2,128,2560]{2,1,0:T(8,128)(2,1)} %bitcast.8, f32[2560]{0:T(1024)} %gain_q_hbm.1, f32[2560]{0:T(1024)} %gain_k_hbm.1, s32[18,256]{1,0:T(8,128)} %bitcast.9, ...), custom_call_target="tpu_custom_call" | custom-call | tf_op jit(solution)/shard_map/pallas_call | solution.py:530
  106.2 1.1 copy.10

commit v8 on v7

--- a/solution.py
+++ b/solution.py
@@ -32,15 +32,15 @@
         + [("direct", K, q) for q in CHUNKS]
         + [("halve", 0)] + [("spread_v", V, q) for q in CHUNKS]
         + [("pass_on", K, 0), ("ring_rest", 0), ("pass_on", K, 1), ("pass_on", K, 3)]
-        + [("scale", Q), ("own", Q), ("spread_q", 0), ("send", Q)]
-        + [("direct", V, 0), ("pass_on", K, 2), ("direct", V, 1), ("finish", K, 0), ("finish", K, 1)]
-        + [("spread_v", W, q) for q in CHUNKS]
-        + [("direct", V, 3), ("relay", 0), ("finish", K, 3), ("direct", V, 2), ("finish", K, 2)]
-        + [("pick", 0), ("pass_on", V, 0), ("direct", W, 0), ("complete", K), ("weigh", 0)]
-        + [("pass_on", V, 1), ("direct", W, 1), ("weigh", 1), ("pass_on", V, 3), ("direct", W, 3), ("weigh", 2)]
-        + [("pass_on", V, 2), ("direct", W, 2), ("weigh", 3), ("finish", V, 0), ("finish", V, 1), ("weigh", 4)]
-        + [("attend", 0), ("pass_on", W, 0), ("finish", V, 3), ("weigh", 5), ("finish", V, 2), ("weigh", 6), ("weigh", 7)]
-        + [("pass_on", W, 1), ("pass_on", W, 3), ("pass_on", W, 2), ("answer", 0)]
+        + [("scale", Q), ("own", Q), ("spread_q", 0), ("send", Q), ("relay", 0)]
+        + [("direct", V, 0), ("pass_on", K, 2), ("direct", V, 1)] + [("spread_v", W, q) for q in CHUNKS]
+        + [("finish", K, 0), ("pick", 0), ("finish", K, 1)]
+        + [("direct", V, 3), ("finish", K, 3), ("direct", V, 2), ("finish", K, 2)]
+        + [("pass_on", V, 0), ("direct", W, 0), ("pass_on", V, 1), ("direct", W, 1)]
+        + [("complete", K), ("weigh", 0), ("pass_on", V, 3), ("direct", W, 3), ("weigh", 1), ("weigh", 2)]
+        + [("pass_on", V, 2), ("direct", W, 2), ("attend", 0), ("weigh", 3), ("finish", V, 0), ("finish", V, 1)]
+        + [("pass_on", W, 0), ("weigh", 4), ("finish", V, 3), ("weigh", 5), ("finish", V, 2)]
+        + [("pass_on", W, 1), ("weigh", 6), ("pass_on", W, 3), ("weigh", 7), ("pass_on", W, 2), ("answer", 0)]
         + [("complete", V), ("mix", V, 0), ("finish", W, 0), ("mix", V, 1)]
         + [("finish", W, 1), ("finish", W, 3), ("finish", W, 2)]
         + [("complete", W), ("mix", W, 0), ("mix", W, 1), ("join", 0)]

time: 107 us -> 107 us (level)
  no operation moved by 1% of the time
where the time goes in v8:
time: 107 us; the launch traced here: 106 us
  Pallas kernels  105 us (98%)
    pallas_call x1, Pallas kernels, on_device(): pl.pallas_call(functools.partial(kernel, n_head), out_shape=pltpu.VMEM(sh...  105 us

profile of v8, /device:TPU:1, one launch (start us, length us, event | category | flops | bytes accessed | tf_op | source)
XLA Modules:
  0.0 106.5 jit_solution(16409403018628173866)
XLA Ops:
  0.0 105.4 %shard_map.82 = bf16[2,128,2560]{2,1,0:T(8,128)(2,1)S(1)} custom-call(s32[256]{0:T(256)} %valid_hbm.1, bf16[2,128,2560]{2,1,0:T(8,128)(2,1)} %bitcast.6, bf16[2,128,2560]{2,1,0:T(8,128)(2,1)} %bitcast.7, bf16[2,128,2560]{2,1,0:T(8,128)(2,1)} %bitcast.8, f32[2560]{0:T(1024)} %gain_q_hbm.1, f32[2560]{0:T(1024)} %gain_k_hbm.1, s32[18,256]{1,0:T(8,128)} %bitcast.9, ...), custom_call_target="tpu_custom_call" | custom-call | tf_op jit(solution)/shard_map/pallas_call | solution.py:530
  105.4 1.1 copy.10

commit v9 on v8

--- a/solution.py
+++ b/solution.py
@@ -21,6 +21,7 @@
 HOPS = ((2, 0), (2, 1), (1, 0), (3, 0), (1, 1), (3, 1), (0, 1))
 CHUNKS = (0, 1, 3, 2)
 GROUPS = 8
+TURNS = 4
 K, V, Q, W = 0, 1, 2, 3
 HALF = HD // 2
 
@@ -41,9 +42,9 @@
         + [("pass_on", V, 2), ("direct", W, 2), ("attend", 0), ("weigh", 3), ("finish", V, 0), ("finish", V, 1)]
         + [("pass_on", W, 0), ("weigh", 4), ("finish", V, 3), ("weigh", 5), ("finish", V, 2)]
         + [("pass_on", W, 1), ("weigh", 6), ("pass_on", W, 3), ("weigh", 7), ("pass_on", W, 2), ("answer", 0)]
-        + [("complete", V), ("mix", V, 0), ("finish", W, 0), ("mix", V, 1)]
-        + [("finish", W, 1), ("finish", W, 3), ("finish", W, 2)]
-        + [("complete", W), ("mix", W, 0), ("mix", W, 1), ("join", 0)]
+        + [("complete", V), ("mix", V, 0), ("mix", V, 1), ("finish", W, 0), ("mix", V, 2)]
+        + [("finish", W, 1), ("mix", V, 3), ("finish", W, 3), ("finish", W, 2)]
+        + [("complete", W)] + [("mix", W, turn) for turn in range(TURNS)] + [("join", 0)]
     )
 
 
@@ -358,7 +359,7 @@
                 both = pltpu.roll(low, HALF, 1) + high
             return both * inverse[block, part]
 
-        @pl.loop(turn * COLUMNS // 2, (turn + 1) * COLUMNS // 2)
+        @pl.loop(turn * COLUMNS // TURNS, (turn + 1) * COLUMNS // TURNS)
         def _(step):
             off = 5 * (step + 1) % COLUMNS
             dz, dy = off // SIDE, off % SIDE

time: 107 us -> 107 us (level)
  no operation moved by 1% of the time
where the time goes in v9:
time: 107 us; the launch traced here: 106 us
  Pallas kernels  105 us (98%)
    pallas_call x1, Pallas kernels, on_device(): pl.pallas_call(functools.partial(kernel, n_head), out_shape=pltpu.VMEM(sh...  105 us

profile of v9, /device:TPU:1, one launch (start us, length us, event | category | flops | bytes accessed | tf_op | source)
XLA Modules:
  0.0 106.5 jit_solution(4867208629956620798)
XLA Ops:
  0.0 105.4 %shard_map.82 = bf16[2,128,2560]{2,1,0:T(8,128)(2,1)S(1)} custom-call(s32[256]{0:T(256)} %valid_hbm.1, bf16[2,128,2560]{2,1,0:T(8,128)(2,1)} %bitcast.6, bf16[2,128,2560]{2,1,0:T(8,128)(2,1)} %bitcast.7, bf16[2,128,2560]{2,1,0:T(8,128)(2,1)} %bitcast.8, f32[2560]{0:T(1024)} %gain_q_hbm.1, f32[2560]{0:T(1024)} %gain_k_hbm.1, s32[18,256]{1,0:T(8,128)} %bitcast.9, ...), custom_call_target="tpu_custom_call" | custom-call | tf_op jit(solution)/shard_map/pallas_call | solution.py:531
  105.4 1.1 copy.10
